TPU v7x, 512 devices: a whole 4x8x8 slice. The times are simulated.
512 devices in a mesh: section: 16 (over x, y_lo, core), dp: 32 (over y_hi, z).
Axes of the slice: x: 4, y: 8 (y_hi: 4, y_lo: 2; y = y_hi * 2 + y_lo), z: 8, core: 2. Of those that a mesh axis runs over, the one named last changes fastest.
Arguments:
- hidden: bfloat16 [196608, 5120], P(('section', 'dp')), may hold values from -6 to 6
- targets: int32 [196608], P(('section', 'dp')), may hold values from 0 to 191
- head_weight: bfloat16 [5120, 192], P('section'), may hold values from -0.25155765 to 0.25155765
- norm_gain: float32 [5120], replicated, may hold values from 0.5 to 1.5
Outputs:
- weight_grad: float32 [5120, 192], P(('section', 'dp'))
- gain_grad: float32 [5120], replicated
All inputs are finite; a program needn't handle non-finite values.
Results may differ from a plain program's by a relative error of at most 0.0029.
Values may be sent and summed in bfloat16 or wider, within the bound.
A program may use at most 64 MiB of HBM per device.

v0:
```python
import jax
import jax.numpy as jnp
from jax import lax
from jax.sharding import PartitionSpec as P

TOK_DEV = 384


def on_device(hidden, targets, head_weight, norm_gain):
    values = hidden.astype(jnp.float32)
    meansq = jnp.mean(values * values, axis=-1, keepdims=True)
    normed = values * lax.rsqrt(meansq + 1e-05)
    scaled = (normed * norm_gain[None, :]).astype(jnp.bfloat16)
    vocab = head_weight.shape[1]
    columns = scaled
    logits = jnp.dot(
        columns,
        lax.all_gather(head_weight, "section", axis=0, tiled=True),
        preferred_element_type=jnp.float32,
    )
    probs = jax.nn.softmax(logits, axis=-1)
    onehot = (targets[:, None] == jnp.arange(vocab, dtype=jnp.int32)[None, :]).astype(jnp.float32)
    dlogits = ((probs - onehot) * (1.0 / TOK_DEV**0.5)).astype(jnp.bfloat16)
    dscaled = jnp.einsum(
        "tv,dv->td",
        dlogits,
        lax.all_gather(head_weight, "section", axis=0, tiled=True),
        preferred_element_type=jnp.float32,
    )
    gain_grad = lax.psum(jnp.sum(dscaled * normed, axis=0), ("section", "dp"))
    columns = scaled
    section_rows = lax.psum_scatter(
        jnp.einsum("td,tv->dv", columns, dlogits, preferred_element_type=jnp.float32),
        "section",
        scatter_dimension=0,
        tiled=True,
    )
    weight_grad = lax.psum_scatter(section_rows, "dp", scatter_dimension=0, tiled=True)
    return (weight_grad, gain_grad)


def solution(mesh):
    placed = (P(("section", "dp"), None), P(("section", "dp")), P("section", None), P())
    return jax.shard_map(
        on_device,
        mesh=mesh,
        in_specs=placed,
        out_specs=(P(("section", "dp"), None), P()),
        check_vma=False,
    )
```

profile of v0, /device:TPU:2, one launch (start us, length us, event | category | flops | bytes accessed | tf_op | source)
XLA Modules:
  0.0 449.6 jit_solution(3670519580004448576)
XLA Ops:
  7.2 0.0 all-gather.3.cloned.1.call-start
  7.2 0.7 all-gather.3.cloned.1.call-update
  7.9 0.0 reduce-scatter.5.cloned.1.call-start
  7.9 3.0 fusion.4
  10.9 0.0 copy-start.2
  10.9 43.1 %all-gather.3.cloned.1.call-done = bf16[16,320,192]{1,2,0:T(8,128)(2,1)} async-done(((bf16[1,320,192]{1,2,0:T(8,128)(2,1)}), bf16[16,320,192]{1,2,0:T(8,128)(2,1)}) %all-gather.3.cloned.1.call-update) | async-done | bytes 1966096 | tf_op jit(solution)/shard_map/all_gather | solution.py:18
  54.1 3.0 copy.9
  57.1 3.0 reshape.17
  60.1 0.0 copy-done.2
  60.1 0.0 copy-start
  60.1 0.0 copy-start.3
  60.1 4.4 fusion.10
  64.5 0.1 fusion.9
  64.6 0.0 copy-done
  64.6 0.0 copy-done.3
  64.6 4.6 %fusion.5 = f32[5120,192]{1,0:T(8,128)} fusion(bf16[384,5120]{1,0:T(8,128)(2,1)S(1)} %copy-done, f32[5120]{0:T(1024)S(1)} %copy-done.2, f32[384]{0:T(512)S(1)} %add_rsqrt_fusion, f32[384,192]{0,1:T(8,128)S(1)} %get-tuple-element.9, s32[384]{0:T(512)S(1)} %copy-done.3, f32[384]{0:T(512)S(1)} %fusion.9, f32[384]{0:T(512)S(1)} %get-tuple-element.8), kind=kOutput, calls=%fused_computation.7 | convolution fusion | flops 763355136 | bytes 8185856
  69.2 0.0 copy-start.1
  69.2 0.0 reduce-scatter.5.cloned.1.call-update
  69.3 0.0 all-reduce.3.cloned.1.call-start
  69.3 1.4 dynamic-slice
  71.4 69.2 %reduce-scatter.5.cloned.1.call-done = f32[320,192]{1,0:T(8,128)} async-done(((f32[5120,192]{1,0:T(8,128)}), f32[320,192]{1,0:T(8,128)}) %reduce-scatter.5.cloned.1.call-update) | async-done | bytes 245776
  140.6 1.8 copy.12
  142.4 0.0 all-reduce.3.cloned.1.call-update
  142.4 0.0 copy-done.1
  142.4 3.5 fusion.3
  145.9 106.8 %psum.7 = f32[5120]{0:T(1024)} all-reduce(f32[5120]{0:T(1024)S(1)} %fusion.3), channel_id=1, replica_groups=mesh['section'=16,'dp'=32] {'section','dp'}, use_global_device_ids=true, to_apply=%region_6.0 | all-reduce | flops 5120 | bytes 40960 | tf_op jit(solution)/shard_map/psum | solution.py:30
  252.7 188.6 %all-reduce.3.cloned.1.call-done = f32[320,192]{0,1:T(8,128)} async-done(((f32[320,192]{0,1:T(8,128)}), f32[320,192]{0,1:T(8,128)}) %all-reduce.3.cloned.1.call-update) | async-done | bytes 245776
  441.4 1.0 constant_dynamic-slice_fusion
  442.4 0.7 copy.10
  (1 shorter events, 0.0 us)
Async XLA Ops:
  7.2 46.9 %all-gather.3.cloned.1.call-start = ((), (), s32[]{:S(2)}) async-start(), calls=%async_computation.1 | async-start | bytes 2506752 | tf_op jit(solution)/shard_map/all_gather | solution.py:18
  7.9 132.7 %reduce-scatter.5.cloned.1.call-start = ((), (), s32[]{:S(2)}) async-start(), calls=%async_computation.2 | async-start | bytes 5570560
  10.9 49.2 %copy-start.2 = (f32[5120]{0:T(1024)S(1)}, f32[5120]{0:T(1024)}, u32[]{:S(2)}) copy-start(f32[5120]{0:T(1024)} %param.7) | copy-start | bytes 61444
  60.1 4.5 %copy-start = (bf16[384,5120]{1,0:T(8,128)(2,1)S(1)}, bf16[384,5120]{1,0:T(8,128)(2,1)}, u32[]{:S(2)}) copy-start(bf16[384,5120]{1,0:T(8,128)(2,1)} %param.4) | copy-start | bytes 11796484
  60.1 4.5 %copy-start.3 = (s32[384]{0:T(512)S(1)}, s32[384]{0:T(512)}, u32[]{:S(2)}) copy-start(s32[384]{0:T(512)} %param.5) | copy-start | bytes 4612
  69.2 73.2 %copy-start.1 = (bf16[5120,192]{0,1:T(8,128)(2,1)S(1)}, bf16[5120,192]{0,1:T(8,128)(2,1)}, u32[]{:S(2)}) copy-start(bf16[5120,192]{0,1:T(8,128)(2,1)} %reshape.17) | copy-start | bytes 5898244
  69.3 372.1 %all-reduce.3.cloned.1.call-start = ((), (), s32[]{:S(2)}) async-start(), calls=%async_computation.3 | async-start | bytes 589824
Sparse Core Ops, SparseCore 0:
  10.1 43.8 all-gather.2
  69.4 71.1 reduce-scatter.4
  143.5 297.8 all-reduce.2
where the time goes:
time: 450 us
  waiting for transfers between devices  302 us (67%)
  blocking collectives  107 us (24%)
  between operations  14.4 us (3%)
  matrix products  12.5 us (3%)
  local copies, waits for them, and re-layouts  11 us (2%)
    unnamed x5, waiting for transfers between devices  259 us
    psum x1, blocking collectives, on_device(): gain_grad = lax.psum(jnp.sum(dscaled * normed, axis=0), ('section', 'dp'))  107 us
    all_gather x1, waiting for transfers between devices, on_device(): lax.all_gather(head_weight, 'section', axis=0, tiled=True)  43.1 us
  transfers between devices with their start and end apart: 3, of which 3 were waited for; matrix products, arithmetic and copies ran while one was open for 2% of the time, Pallas kernels for 0%

commit v1 on v0

v1 whole, which is shorter than its diff:
```python
import jax
import jax.numpy as jnp
from jax import lax
from jax.experimental import pallas as pl
from jax.experimental.pallas import tpu as pltpu
from jax.sharding import PartitionSpec as P

D = 5120
V = 192
TOK = 384
NX, NY, NZ = 4, 8, 8
QW = 640
MESH = pl.DeviceIdType.MESH
F32 = jnp.float32
BF16 = jnp.bfloat16
SCALE = 1.0 / TOK**0.5


def kernel(
    hid, tgt, w, gain, wg_out, gg_out,
    h, s, rv, wp, wu, logit, dlz, dle,
    a_keep, a_send, a_core, b_keep, b_send, b_core,
    ax_send, ax_recv, a_acc, ay_send, ay_recv, a_fin, az_send, az_recv,
    by_send, by_acc, by_recv, bx_send, bx_recv, b_fin, bz_send, bz_recv,
    g_loc, g_core, g_x, g_y, g_z, g_mine, g_full,
    hsem,
    wx_s, wx_r, wy_s, wy_r, wc_s, wc_r,
    ac_s, ac_r, bc_s, bc_r,
    ax_s, ax_r, ay_s, ay_r, az_s, az_r,
    by_s, by_r, bx_s, bx_r, bz_s, bz_r,
    gc_s, gc_r, gx_s, gx_r, gy_s, gy_r, gz_s, gz_r, gf_s, gf_r,
):
    sec = lax.axis_index("section")
    dp = lax.axis_index("dp")
    c = lax.rem(sec, 2)
    yl = lax.rem(lax.div(sec, 2), 2)
    x = lax.div(sec, 4)
    yh = lax.div(dp, NZ)
    z = lax.rem(dp, NZ)
    y = yh * 2 + yl
    oc = 1 - c

    def dev(x_, y_, z_, c_):
        return (x_ * 4 + lax.rem(y_, 2) * 2 + c_, lax.div(y_, 2) * NZ + z_)

    def xo(k):
        return lax.rem(x + k, NX)

    def yo(k):
        return lax.rem(y + k, NY)

    def zo(k):
        return lax.rem(z + k, NZ)

    def rcopy(src, dst, ss, rs, to):
        return pltpu.make_async_remote_copy(
            src_ref=src, dst_ref=dst, send_sem=ss, recv_sem=rs,
            device_id=to, device_id_type=MESH)

    hcopies = [
        pltpu.make_async_copy(hid.at[pl.ds(96 * i, 96)], h.at[pl.ds(96 * i, 96)], hsem.at[i])
        for i in range(4)
    ]
    for cp in hcopies:
        cp.start()

    barrier = pltpu.get_barrier_semaphore()
    peers = [dev(xo(k), y, z, c) for k in range(1, NX)]
    peers += [dev(x, yo(k), z, c) for k in range(1, NY)]
    peers += [dev(x, y, zo(k), c) for k in range(1, NZ)]
    peers += [dev(x, y, zo(k), oc) for k in range(NZ)]
    for p in peers:
        pl.semaphore_signal(barrier, inc=1, device_id=p, device_id_type=MESH)

    wp[sec, 0:320, :] = w[:, 0:128]
    wp[sec, 320:480, :] = jnp.concatenate([w[0:160, 128:192], w[160:320, 128:192]], axis=1)

    t_row = tgt[...].astype(F32)
    t_col = jnp.transpose(jnp.broadcast_to(t_row.reshape(1, TOK), (128, TOK)))

    pl.semaphore_wait(barrier, len(peers))

    started = []

    def go(cp):
        cp.start()
        started.append(cp)
        return cp

    wx = [None] * NX
    for k in (1, 3, 2):
        wx[k] = go(rcopy(wp.at[sec], wp.at[sec], wx_s.at[k], wx_r.at[k], dev(xo(k), y, z, c)))

    def shard(k, l, cc):
        return xo(NX - k if k else 0) * 4 + l * 2 + cc

    def fwd_y(k):
        sh = shard(k, yl, c)
        lo = go(rcopy(wp.at[sh, pl.ds(0, 240)], wp.at[sh, pl.ds(0, 240)],
                      wy_s.at[k, 0], wy_r.at[k, 0], dev(x, yo(1), z, c)))
        hi = go(rcopy(wp.at[sh, pl.ds(240, 240)], wp.at[sh, pl.ds(240, 240)],
                      wy_s.at[k, 1], wy_r.at[k, 1], dev(x, yo(NY - 1), z, c)))
        return lo, hi

    def fwd_c(k, j):
        sh = shard(k, yl if j == 0 else 1 - yl, c)
        return go(rcopy(wp.at[sh], wp.at[sh], wc_s.at[k, j], wc_r.at[k, j], dev(x, y, z, oc)))

    wy = {0: fwd_y(0)}
    wc = {(0, 0): fwd_c(0, 0)}

    def rows(i, carry):
        r0 = pl.multiple_of(i * 16, 16)
        acc = jnp.zeros((16, 128), F32)
        for j in range(D // 128):
            v = h[pl.ds(r0, 16), j * 128:(j + 1) * 128].astype(F32)
            acc = acc + v * v
        ms = jnp.sum(acc, axis=1, keepdims=True) * (1.0 / D)
        r = jnp.broadcast_to(lax.rsqrt(ms + 1e-05), (16, 128))
        rv[pl.ds(r0, 16), :] = r
        for j in range(D // 128):
            v = h[pl.ds(r0, 16), j * 128:(j + 1) * 128].astype(F32)
            gj = gain[:, j * 128:(j + 1) * 128]
            s[pl.ds(r0, 16), j * 128:(j + 1) * 128] = ((v * r) * gj).astype(BF16)
        return carry

    def quarter(i):
        hcopies[i].wait()
        lax.fori_loop(6 * i, 6 * i + 6, rows, 0)

    quarter(0)
    quarter(1)
    for n, k in enumerate((1, 3, 2)):
        wx[k].wait_recv()
        wy[k] = fwd_y(k)
        wc[(k, 0)] = fwd_c(k, 0)
        if n < 2:
            quarter(2 + n)

    def unpack(k, j):
        l = yl if j == 0 else 1 - yl
        q = xo(NX - k if k else 0) * 2 + l
        for cc in range(2):
            sh = q * 2 + cc
            wu[q, cc * 320:(cc + 1) * 320, 0:128] = wp[sh, 0:320, :]
            b = wp[sh, 320:480, :]
            wu[q, cc * 320:cc * 320 + 160, 128:256] = b
            wu[q, cc * 320 + 160:(cc + 1) * 320, 128:256] = pltpu.roll(
                b.astype(F32), 64, 1).astype(BF16)
        return q

    def add_logits(k, j):
        wc[(k, j)].wait_recv()
        q = unpack(k, j)
        part = jnp.dot(s[:, pl.ds(pl.multiple_of(q * QW, 128), QW)], wu[q],
                       preferred_element_type=F32)
        if (k, j) == (0, 0):
            logit[...] = part
        else:
            logit[...] += part

    add_logits(0, 0)

    def take_y(k):
        wy[k][0].wait_recv()
        wy[k][1].wait_recv()
        wc[(k, 1)] = fwd_c(k, 1)

    order = (0, 1, 3, 2)
    take_y(0)
    take_y(1)
    add_logits(1, 0)
    add_logits(3, 0)
    take_y(3)
    add_logits(0, 1)
    add_logits(2, 0)
    take_y(2)
    add_logits(1, 1)
    add_logits(3, 1)
    add_logits(2, 1)

    lane = lax.broadcasted_iota(jnp.int32, (TOK, 256), 1)
    lg = jnp.where(lane < V, logit[...], -3e38)
    m = jnp.max(lg, axis=1, keepdims=True)
    e = jnp.where(lane < V, jnp.exp(lg - m), 0.0)
    p = e / jnp.sum(e, axis=1, keepdims=True)
    tc = jnp.concatenate([t_col, t_col], axis=1)
    onehot = (tc == lane.astype(F32)).astype(F32)
    dl = ((p - onehot) * SCALE).astype(BF16)
    dlz[...] = dl
    up = dl[:, 128:256].astype(F32)
    dle[:, 0:128] = dl[:, 0:128]
    dle[:, 128:256] = (up + pltpu.roll(up, 64, 1)).astype(BF16)

    lane_lo = lax.broadcasted_iota(jnp.int32, (320, 128), 1) < 64
    xorder = (1, 3, 2, 0)
    part_dev = dev(x, y, z, oc)

    ac = {}
    bcp = {}
    for k in xorder:
        xx = xo(k)
        for l in range(2):
            q = xx * 2 + l
            wv = lax.dot_general(
                s[:, pl.ds(pl.multiple_of(q * QW, 128), QW)], dle[...],
                (((0,), (0,)), ((), ())), preferred_element_type=F32)
            top, bot = wv[0:320, 0:128], wv[320:640, 0:128]
            a_send[xx, l] = jnp.where(c == 0, bot, top).astype(BF16)
            ac[(k, l)] = go(rcopy(a_send.at[xx, l], a_core.at[xx, l],
                                  ac_s.at[k, l], ac_r.at[k, l], part_dev))
            a_keep[xx, l] = jnp.where(c == 0, top, bot)
            bq = jnp.where(lane_lo, wv[0:320, 128:256], wv[320:640, 128:256])
            b_keep[xx, l] = bq
            b_send[xx, l] = bq.astype(BF16)
            bcp[(k, l)] = rcopy(b_send.at[xx, l], b_core.at[xx, l],
                                bc_s.at[k, l], bc_r.at[k, l], part_dev)

            @pl.when(lax.div(xx, 2) != c)
            def _():
                bcp[(k, l)].start()

    ax = {}
    byc = {}
    for k in xorder:
        xx = xo(k)
        for l in range(2):
            ac[(k, l)].wait_recv()
            tot = a_keep[xx, l] + a_core[xx, l].astype(F32)
            if k:
                ax_send[k - 1, l] = tot.astype(BF16)
                ax[(k, l)] = go(rcopy(ax_send.at[k - 1, l], ax_recv.at[k - 1, l],
                                      ax_s.at[k, l], ax_r.at[k, l], dev(xx, y, z, c)))
            else:
                a_acc[l] = tot
        bi = lax.rem(xx, 2)
        for j in range(1, NY):
            yy = yo(j)
            byc[(k, j)] = rcopy(by_send.at[bi, lax.rem(yy, 2), pl.ds(pl.multiple_of(lax.div(yy, 2) * 80, 16), 80)],
                                by_recv.at[bi, j - 1],
                                by_s.at[bi, j], by_r.at[bi, j], dev(x, yy, z, c))

        @pl.when(lax.div(xx, 2) == c)
        def _():
            for l in range(2):
                bcp[(k, l)].wait_recv()
                tot = b_keep[xx, l] + b_core[xx, l].astype(F32)
                by_acc[bi, l] = tot
                by_send[bi, l] = tot.astype(BF16)
            for j in range(1, NY):
                byc[(k, j)].start()

    def gain_chunk(q, carry):
        cols = pl.ds(pl.multiple_of(q * QW, 128), QW)
        ds = lax.dot_general(dlz[...], wu[q], (((1,), (1,)), ((), ())),
                             preferred_element_type=F32)
        n = h[:, cols].astype(F32) * jnp.concatenate([rv[...]] * 5, axis=1)
        g_loc[pl.ds(q, 1), :] = jnp.sum(ds * n, axis=0, keepdims=True)
        return carry

    lax.fori_loop(0, 8, gain_chunk, 0)
    glane = pl.multiple_of(c * 256, 128)
    golane = pl.multiple_of(oc * 256, 128)
    gc = go(rcopy(g_loc.at[:, pl.ds(golane, 384)], g_core, gc_s, gc_r, part_dev))

    ay = {}
    for l in range(2):
        tot = a_acc[l]
        for k in (1, 3, 2):
            ax[(k, l)].wait_recv()
            tot = tot + ax_recv[k - 1, l].astype(F32)
        a_acc[l] = tot
        ay_send[l] = tot.astype(BF16)
    for j in range(1, NY):
        yy = yo(j)
        ay[j] = go(rcopy(ay_send.at[lax.rem(yy, 2), pl.ds(pl.multiple_of(lax.div(yy, 2) * 80, 16), 80)],
                         ay_recv.at[j - 1], ay_s.at[j], ay_r.at[j], dev(x, yy, z, c)))

    def spread(buf, own, stage_s, stage_r, count, to):
        cps = []
        for k in range(1, count):
            cps.append(go(rcopy(buf.at[own], buf.at[own], stage_s.at[k], stage_r.at[k], to(k))))
        return cps

    gc.wait_recv()
    g_x[x] = g_loc[:, pl.ds(glane, 384)] + g_core[...]
    gx = spread(g_x, x, gx_s, gx_r, NX, lambda k: dev(xo(k), y, z, c))

    for b in range(2):
        tot = by_acc[b, yl, pl.ds(pl.multiple_of(yh * 80, 16), 80)]
        for j in range(1, NY):
            pltpu.make_async_copy(by_recv.at[b, j - 1], by_recv.at[b, j - 1], by_r.at[b, j]).wait()
            tot = tot + by_recv[b, j - 1].astype(F32)
        bx_send[b] = tot
    mine = lax.div(x, 2) == c
    bx = {}
    for k in range(1, NX):
        xx = xo(k)
        bx[k] = rcopy(bx_send.at[lax.rem(xx, 2)], bx_recv.at[k - 1],
                      bx_s.at[k], bx_r.at[k], dev(xx, y, z, c))

        @pl.when(lax.div(xx, 2) == c)
        def _():
            bx[k].start()

    for cp in gx:
        cp.wait_recv()
    g_y[y] = (g_x[0] + g_x[1]) + (g_x[2] + g_x[3])
    gy = spread(g_y, y, gy_s, gy_r, NY, lambda k: dev(x, yo(k), z, c))

    tot = a_acc[yl, pl.ds(pl.multiple_of(yh * 80, 16), 80)]
    for j in range(1, NY):
        ay[j].wait_recv()
        tot = tot + ay_recv[j - 1].astype(F32)
    a_fin[0:80] = tot
    for i in range(NZ):
        az_send[i] = a_fin[10 * i:10 * i + 16]
    az = {}
    for k in range(1, NZ):
        zz = zo(k)
        az[k] = go(rcopy(az_send.at[zz], az_recv.at[k], az_s.at[k], az_r.at[k], dev(x, y, zz, c)))

    bz = {}
    for k in range(NZ):
        zz = zo(k)
        for o in range(0 if k else 1, 2):
            bz[(k, o)] = rcopy(bz_send.at[zz], bz_recv.at[k], bz_s.at[k, o], bz_r.at[k],
                               dev(x, y, zz, c if o == 0 else oc))

    @pl.when(mine)
    def _():
        t = bx_send[lax.rem(x, 2)]
        for k in (1, 3, 2):
            bx[k].wait_recv()
            t = t + bx_recv[k - 1]
        b_fin[0:80] = t
        for i in range(NZ):
            bz_send[i] = b_fin[10 * i:10 * i + 16]
        bz_recv[0] = bz_send[z]
        for k in range(NZ):
            for o in range(0 if k else 1, 2):
                bz[(k, o)].start()

    for cp in gy:
        cp.wait_recv()
    g_z[z] = ((g_y[0] + g_y[1]) + (g_y[2] + g_y[3])) + ((g_y[4] + g_y[5]) + (g_y[6] + g_y[7]))
    gz = spread(g_z, z, gz_s, gz_r, NZ, lambda k: dev(x, y, zo(k), c))

    ta = az_send[z]
    for k in range(1, NZ):
        az[k].wait_recv()
        ta = ta + az_recv[k]
    wg_out[:, 0:128] = ta[0:10]

    @pl.when(jnp.logical_not(mine))
    def _():
        bz[(0, 1)].wait_recv()

    tb = bz_recv[0]
    for k in range(1, NZ):
        bz[(k, 0)].wait_recv()
        tb = tb + bz_recv[k]
    tb = jnp.where(c == 0, tb, pltpu.roll(tb, 64, 1))
    wg_out[:, 128:192] = tb[0:10, 0:64]

    for cp in gz:
        cp.wait_recv()
    g_mine[...] = ((g_z[0] + g_z[1]) + (g_z[2] + g_z[3])) + ((g_z[4] + g_z[5]) + (g_z[6] + g_z[7]))
    gf = go(rcopy(g_mine, g_full, gf_s, gf_r, part_dev))
    gf.wait_recv()

    @pl.when(c == 0)
    def _():
        gg_out[:, 0:384] = g_mine[...]
        gg_out[:, 384:640] = g_full[:, 128:384]

    @pl.when(c == 1)
    def _():
        gg_out[:, 0:256] = g_full[:, 0:256]
        gg_out[:, 256:640] = g_mine[...]

    for cp in started:
        cp.wait_send()
    for k in range(NX):
        xx = xo(k)

        @pl.when(lax.div(xx, 2) != c)
        def _():
            for l in range(2):
                bcp[(k, l)].wait_send()

        @pl.when(lax.div(xx, 2) == c)
        def _():
            for j in range(1, NY):
                byc[(k, j)].wait_send()
            if k:
                bx[k].wait_send()

    @pl.when(mine)
    def _():
        for k in range(NZ):
            for o in range(0 if k else 1, 2):
                bz[(k, o)].wait_send()


def on_device(hidden, targets, head_weight, norm_gain):
    dma = pltpu.SemaphoreType.DMA
    vm = pltpu.VMEM
    scratch = [
        vm((TOK, D), BF16), vm((TOK, D), BF16), vm((TOK, 128), F32),
        vm((16, 480, 128), BF16), vm((8, QW, 256), BF16),
        vm((TOK, 256), F32), vm((TOK, 256), BF16), vm((TOK, 256), BF16),
        vm((4, 2, 320, 128), F32), vm((4, 2, 320, 128), BF16), vm((4, 2, 320, 128), BF16),
        vm((4, 2, 320, 128), F32), vm((4, 2, 320, 128), BF16), vm((4, 2, 320, 128), BF16),
        vm((3, 2, 320, 128), BF16), vm((3, 2, 320, 128), BF16), vm((2, 320, 128), F32),
        vm((2, 320, 128), BF16), vm((7, 80, 128), BF16),
        vm((96, 128), F32), vm((8, 16, 128), F32), vm((8, 16, 128), F32),
        vm((2, 2, 320, 128), BF16), vm((2, 2, 320, 128), F32), vm((2, 7, 80, 128), BF16),
        vm((2, 80, 128), F32), vm((3, 80, 128), F32),
        vm((96, 128), F32), vm((8, 16, 128), F32), vm((8, 16, 128), F32),
        vm((8, QW), F32), vm((8, 384), F32), vm((4, 8, 384), F32),
        vm((8, 8, 384), F32), vm((8, 8, 384), F32), vm((8, 384), F32), vm((8, 384), F32),
        dma((4,)),
        dma((4,)), dma((4,)), dma((4, 2)), dma((4, 2)), dma((4, 2)), dma((4, 2)),
        dma((4, 2)), dma((4, 2)), dma((4, 2)), dma((4, 2)),
        dma((4, 2)), dma((4, 2)), dma((8,)), dma((8,)), dma((8,)), dma((8,)),
        dma((2, 8)), dma((2, 8)), dma((4,)), dma((4,)), dma((8, 2)), dma((8,)),
        dma, dma, dma((4,)), dma((4,)), dma((8,)), dma((8,)), dma((8,)), dma((8,)), dma, dma,
    ]
    vspec = pl.BlockSpec(memory_space=pltpu.VMEM)
    wg, gg = pl.pallas_call(
        kernel,
        out_shape=(jax.ShapeDtypeStruct((10, V), F32), jax.ShapeDtypeStruct((8, QW), F32)),
        in_specs=[pl.BlockSpec(memory_space=pl.ANY), vspec, vspec, vspec],
        out_specs=(vspec, vspec),
        scratch_shapes=scratch,
        compiler_params=pltpu.CompilerParams(
            collective_id=0, has_side_effects=True, vmem_limit_bytes=56 * 1024 * 1024),
        cost_estimate=pl.CostEstimate(flops=3 * 2 * TOK * D * V, bytes_accessed=TOK * D * 2,
                                      transcendentals=TOK * V),
    )(hidden, targets.reshape(1, TOK), head_weight, norm_gain.reshape(1, D))
    return wg, gg.reshape(D)


def solution(mesh):
    placed = (P(("section", "dp"), None), P(("section", "dp")), P("section", None), P())
    return jax.shard_map(
        on_device,
        mesh=mesh,
        in_specs=placed,
        out_specs=(P(("section", "dp"), None), P()),
        check_vma=False,
    )
```

time: 450 us -> 68.3 us (0.15)
  the two profiles are of different devices: /device:TPU:2 before, /device:TPU:1 now
where the time goes in v1:
time: 68.3 us; the launch traced here: 68 us
  Pallas kernels  61.8 us (90%)
  local copies, waits for them, and re-layouts  5.59 us (8%)
    pallas_call x1, Pallas kernels, on_device(): pl.pallas_call(kernel, out_shape=(jax.ShapeDtypeStruct((10, V), F32), jax...  61.8 us
    unnamed x2, local copies, waits for them, and re-layouts  3.01 us

profile of v1, /device:TPU:1, one launch (start us, length us, event | category | flops | bytes accessed | tf_op | source)
XLA Modules:
  0.0 68.0 jit_solution(7304965821369592518)
XLA Ops:
  0.6 1.2 %reshape.13.tgt = s32[1,384]{1,0:T(1,128)} reshape(s32[384]{0:T(512)} %param.5) | data formatting | bytes 3072 | tf_op jit(solution)/shard_map/reshape | solution.py:441
  1.9 1.7 %copy.6.w = bf16[320,192]{1,0:T(8,128)(2,1)} copy(bf16[320,192]{0,1:T(8,128)(2,1)} %param.6) | data formatting | bytes 245760 | tf_op args[2]
  3.6 61.8 %shard_map.59 = (f32[10,192]{1,0:T(8,128)}, f32[8,640]{1,0:T(8,128)}) custom-call(bf16[384,5120]{1,0:T(8,128)(2,1)} %hid.1, s32[1,384]{1,0:T(1,128)} %reshape.13.tgt, bf16[320,192]{1,0:T(8,128)(2,1)} %copy.6.w, f32[1,5120]{1,0:T(1,128)} %bitcast.1), custom_call_target="tpu_custom_call" | custom-call | flops 2264924160 | bytes 3932160 | tf_op jit(solution)/shard_map/pallas_call | solution.py:431
  65.3 1.3 %reshape.15 = f32[5120]{0:T(1024)} reshape(f32[8,640]{1,0:T(8,128)} %get-tuple-element.5) | data formatting | bytes 40960 | tf_op jit(solution)/shard_map/reshape | solution.py:442
  66.7 1.3 %copy.8 = f32[10,192]{1,0:T(8,128)} copy(f32[10,192]{1,0:T(8,128)} %get-tuple-element.8) | data formatting | bytes 15360

commit v2 on v1

v2 whole, which is shorter than its diff:
```python
import jax
import jax.numpy as jnp
from jax import lax
from jax.experimental import pallas as pl
from jax.experimental.pallas import tpu as pltpu
from jax.sharding import PartitionSpec as P

D = 5120
V = 192
TOK = 384
NX, NY, NZ = 4, 8, 8
QW = 640
MESH = pl.DeviceIdType.MESH
F32 = jnp.float32
BF16 = jnp.bfloat16
SCALE = 1.0 / TOK**0.5


def kernel(
    hid, tgt, wt, gain, wg_out, gg_out,
    h, s, rv, wp, wu, logit, dlz, dle,
    a_keep, a_send, a_core, b_keep, b_send, b_core,
    ax_send, ax_recv, a_acc, ay_send, ay_recv, a_fin, az_send, az_recv,
    bf_send, bf_acc, bf_recv, bx_send, bx_recv, b_fin, bz_send, bz_recv,
    g_loc, g_core, g_x, g_y, g_z, g_mine, g_full,
    hsem,
    wx_s, wx_r, wy_s, wy_r, wc_s, wc_r,
    ac_s, ac_r, bc_s, bc_r,
    ax_s, ax_r, ay_s, ay_r, az_s, az_r,
    bf_s, bf_r, bx_s, bx_r, bz_s, bz_r,
    gc_s, gc_r, gx_s, gx_r, gy_s, gy_r, gz_s, gz_r, gf_s, gf_r,
):
    sec = lax.axis_index("section")
    dp = lax.axis_index("dp")
    c = lax.rem(sec, 2)
    yl = lax.rem(lax.div(sec, 2), 2)
    x = lax.div(sec, 4)
    yh = lax.div(dp, NZ)
    z = lax.rem(dp, NZ)
    y = yh * 2 + yl
    oc = 1 - c
    odd = lax.rem(x, 2)
    mine = lax.div(x, 2) == c

    def dev(x_, y_, z_, c_):
        return (x_ * 4 + lax.rem(y_, 2) * 2 + c_, lax.div(y_, 2) * NZ + z_)

    def xo(k):
        return lax.rem(x + k, NX)

    def yo(k):
        return lax.rem(y + k, NY)

    def zo(k):
        return lax.rem(z + k, NZ)

    def rcopy(src, dst, ss, rs, to):
        return pltpu.make_async_remote_copy(
            src_ref=src, dst_ref=dst, send_sem=ss, recv_sem=rs,
            device_id=to, device_id_type=MESH)

    hcopies = [
        pltpu.make_async_copy(hid.at[pl.ds(96 * i, 96)], h.at[pl.ds(96 * i, 96)], hsem.at[i])
        for i in range(4)
    ]
    for cp in hcopies:
        cp.start()

    barrier = pltpu.get_barrier_semaphore()
    peers = [dev(x, y, z, oc)]
    peers += [dev(xo(k), y, z, c) for k in range(1, NX)]
    peers += [dev(x, yo(k), z, c) for k in range(1, NY)]
    peers += [dev(x, y, zo(k), c) for k in range(1, NZ)]
    for p in peers:
        pl.semaphore_signal(barrier, inc=1, device_id=p, device_id_type=MESH)

    eye = (lax.broadcasted_iota(jnp.int32, (320, 320), 0)
           == lax.broadcasted_iota(jnp.int32, (320, 320), 1)).astype(BF16)
    w = lax.dot_general(eye, wt[...], (((1,), (1,)), ((), ())), preferred_element_type=F32)
    wp[sec, 0:320, :] = w[:, 0:128].astype(BF16)
    wp[sec, 320:480, :] = jnp.concatenate(
        [w[0:160, 128:192], w[160:320, 128:192]], axis=1).astype(BF16)

    pl.semaphore_wait(barrier, len(peers))

    started = []

    def go(cp):
        cp.start()
        started.append(cp)
        return cp

    def shard(k, l, cc):
        return xo(NX - k if k else 0) * 4 + l * 2 + cc

    def half(sh, i):
        return wp.at[sh, pl.ds(240 * i, 240)]

    wx, wy, wc = {}, {}, {}

    def send_x(k, i):
        wx[(k, i)] = go(rcopy(half(sec, i), half(sec, i), wx_s.at[k, i], wx_r.at[k, i],
                              dev(xo(k), y, z, c)))

    def fwd_y(k, i):
        sh = shard(k, yl, c)
        wy[(k, i)] = go(rcopy(half(sh, i), half(sh, i), wy_s.at[k, i], wy_r.at[k, i],
                              dev(x, yo(NY - 1 if i else 1), z, c)))

    def fwd_c(k, j):
        sh = shard(k, yl if j == 0 else 1 - yl, c)
        wc[(k, j)] = go(rcopy(wp.at[sh], wp.at[sh], wc_s.at[k, j], wc_r.at[k, j], dev(x, y, z, oc)))

    for i in range(2):
        send_x(1, i)
        send_x(3, 1 - i)
        fwd_y(0, i)
    fwd_c(0, 0)

    def rows(i, carry):
        r0 = pl.multiple_of(i * 16, 16)
        acc = jnp.zeros((16, 128), F32)
        for j in range(D // 128):
            v = h[pl.ds(r0, 16), j * 128:(j + 1) * 128].astype(F32)
            acc = acc + v * v
        ms = jnp.sum(acc, axis=1, keepdims=True) * (1.0 / D)
        r = jnp.broadcast_to(lax.rsqrt(ms + 1e-05), (16, 128))
        rv[pl.ds(r0, 16), :] = r
        for j in range(D // 128):
            v = h[pl.ds(r0, 16), j * 128:(j + 1) * 128].astype(F32)
            gj = gain[:, j * 128:(j + 1) * 128]
            s[pl.ds(r0, 16), j * 128:(j + 1) * 128] = ((v * r) * gj).astype(BF16)
        return carry

    def quarter(i):
        hcopies[i].wait()
        lax.fori_loop(6 * i, 6 * i + 6, rows, 0)

    def take_x(k, i):
        wx[(k, i)].wait_recv()
        fwd_y(k, i)

    def take_y(k):
        wy[(k, 0)].wait_recv()
        wy[(k, 1)].wait_recv()
        fwd_c(k, 1)

    def unpack(k, j):
        l = yl if j == 0 else 1 - yl
        q = xo(NX - k if k else 0) * 2 + l
        for cc in range(2):
            sh = q * 2 + cc
            wu[q, cc * 320:(cc + 1) * 320, 0:128] = wp[sh, 0:320, :]
            b = wp[sh, 320:480, :]
            wu[q, cc * 320:cc * 320 + 160, 128:256] = b
            wu[q, cc * 320 + 160:(cc + 1) * 320, 128:256] = pltpu.roll(
                b.astype(F32), 64, 1).astype(BF16)
        return q

    def add_logits(k, j):
        wc[(k, j)].wait_recv()
        q = unpack(k, j)
        part = jnp.dot(s[:, pl.ds(pl.multiple_of(q * QW, 128), QW)], wu[q],
                       preferred_element_type=F32)
        if (k, j) == (0, 0):
            logit[...] = part
        else:
            logit[...] += part

    quarter(0)
    for i in range(2):
        send_x(2, i)
    quarter(1)
    quarter(2)
    take_x(1, 0)
    take_x(3, 1)
    quarter(3)
    take_x(1, 1)
    take_x(3, 0)
    fwd_c(1, 0)
    fwd_c(3, 0)
    add_logits(0, 0)
    take_y(0)
    add_logits(1, 0)
    add_logits(3, 0)
    add_logits(0, 1)
    take_x(2, 0)
    take_x(2, 1)
    fwd_c(2, 0)
    add_logits(2, 0)
    take_y(1)
    take_y(3)
    add_logits(1, 1)
    add_logits(3, 1)
    take_y(2)
    add_logits(2, 1)

    lane = lax.broadcasted_iota(jnp.int32, (TOK, 256), 1)
    t_col = jnp.transpose(jnp.broadcast_to(tgt[...].reshape(1, TOK).astype(F32), (128, TOK)))
    tc = jnp.concatenate([t_col, t_col], axis=1)
    onehot = (tc == lane.astype(F32)).astype(F32)
    lg = jnp.where(lane < V, logit[...], -3e38)
    m = jnp.max(lg, axis=1, keepdims=True)
    e = jnp.where(lane < V, jnp.exp(lg - m), 0.0)
    p = e / jnp.sum(e, axis=1, keepdims=True)
    dl = ((p - onehot) * SCALE).astype(BF16)
    dlz[...] = dl
    up = dl[:, 128:256].astype(F32)
    dle[:, 0:128] = dl[:, 0:128]
    dle[:, 128:256] = (up + pltpu.roll(up, 64, 1)).astype(BF16)

    lane_lo = lax.broadcasted_iota(jnp.int32, (320, 128), 1) < 64
    part_dev = dev(x, y, z, oc)

    ac, bcp, ax = {}, {}, {}

    def chunk(l, k):
        xx = xo(k)
        q = xx * 2 + l
        wv = lax.dot_general(
            s[:, pl.ds(pl.multiple_of(q * QW, 128), QW)], dle[...],
            (((0,), (0,)), ((), ())), preferred_element_type=F32)
        top, bot = wv[0:320, 0:128], wv[320:640, 0:128]
        a_send[xx, l] = jnp.where(c == 0, bot, top).astype(BF16)
        ac[(k, l)] = go(rcopy(a_send.at[xx, l], a_core.at[xx, l],
                              ac_s.at[k, l], ac_r.at[k, l], part_dev))
        bq = jnp.where(lane_lo, wv[0:320, 128:256], wv[320:640, 128:256])
        b_send[xx, l] = bq.astype(BF16)
        bcp[(k, l)] = rcopy(b_send.at[xx, l], b_core.at[xx, l],
                            bc_s.at[k, l], bc_r.at[k, l], part_dev)

        @pl.when(lax.div(xx, 2) != c)
        def _():
            bcp[(k, l)].start()

        a_keep[xx, l] = jnp.where(c == 0, top, bot)
        b_keep[xx, l] = bq

    def chip_sum(l, k):
        xx = xo(k)
        ac[(k, l)].wait_recv()
        tot = a_keep[xx, l] + a_core[xx, l].astype(F32)
        if k:
            ax_send[k - 1, l] = tot.astype(BF16)
            ax[(k, l)] = go(rcopy(ax_send.at[k - 1, l], ax_recv.at[k - 1, l],
                                  ax_s.at[k, l], ax_r.at[k, l], dev(xx, y, z, c)))
        else:
            a_acc[l] = tot
        b = lax.rem(xx, 2)
        at = jnp.where(b == 0, y, z)

        @pl.when(lax.div(xx, 2) == c)
        def _():
            bcp[(k, l)].wait_recv()
            tot = b_keep[xx, l] + b_core[xx, l].astype(F32)
            bf_acc[b, l] = tot
            bf_send[b, l] = tot.astype(BF16)
            for i in range(4):
                g = i * 2 + l
                j = lax.rem(g + 8 - at, 8)

                @pl.when(j != 0)
                def _():
                    rcopy(bf_send.at[b, l, pl.ds(80 * i, 80)], bf_recv.at[b, j],
                          bf_s.at[b, j], bf_r.at[b, j],
                          dev(x, jnp.where(b == 0, g, y), jnp.where(b == 0, z, g), c)).start()

    before = None
    for l in range(2):
        for k in (2, 1, 3, 0):
            chunk(l, k)
            if before:
                chip_sum(*before)
            before = (l, k)
    chip_sum(*before)

    def gain_chunk(q, carry):
        cols = pl.ds(pl.multiple_of(q * QW, 128), QW)
        ds = lax.dot_general(dlz[...], wu[q], (((1,), (1,)), ((), ())),
                             preferred_element_type=F32)
        n = h[:, cols].astype(F32) * jnp.concatenate([rv[...]] * 5, axis=1)
        t = jnp.sum(ds * n, axis=0, keepdims=True)
        for i in range(5):
            g_loc[pl.ds(q * 5 + i, 1), :] = t[:, i * 128:(i + 1) * 128]
        return carry

    lax.fori_loop(0, 8, gain_chunk, 0)
    grow = pl.multiple_of(c * 16, 8)
    gorow = pl.multiple_of(oc * 16, 8)
    gc = go(rcopy(g_loc.at[pl.ds(gorow, 24)], g_core, gc_s, gc_r, part_dev))

    ay = {}

    def x_to_y(l):
        tot = a_acc[l]
        for k in (1, 3, 2):
            ax[(k, l)].wait_recv()
            tot = tot + ax_recv[k - 1, l].astype(F32)
        a_acc[l] = tot
        ay_send[l] = tot.astype(BF16)
        for i in range(4):
            g = i * 2 + l
            j = lax.rem(g + 8 - y, 8)

            @pl.when(j != 0)
            def _():
                rcopy(ay_send.at[l, pl.ds(80 * i, 80)], ay_recv.at[j],
                      ay_s.at[j], ay_r.at[j], dev(x, g, z, c)).start()

    def spread(buf, own, stage_s, stage_r, count, to):
        cps = []
        for k in range(1, count):
            cps.append(go(rcopy(buf.at[own], buf.at[own], stage_s.at[k], stage_r.at[k], to(k))))
        return cps

    def sum8(v):
        return ((v[0] + v[1]) + (v[2] + v[3])) + ((v[4] + v[5]) + (v[6] + v[7]))

    x_to_y(0)

    gc.wait_recv()
    g_x[x] = g_loc[pl.ds(grow, 24)] + g_core[...]
    gx = spread(g_x, x, gx_s, gx_r, NX, lambda k: dev(xo(k), y, z, c))

    x_to_y(1)

    for cp in gx:
        cp.wait_recv()
    g_z[z] = (g_x[0] + g_x[1]) + (g_x[2] + g_x[3])
    gz = spread(g_z, z, gz_s, gz_r, NZ, lambda k: dev(x, y, zo(k), c))

    for b in range(2):
        at = z if b else y
        tot = bf_acc[b, lax.rem(at, 2), pl.ds(pl.multiple_of(lax.div(at, 2) * 80, 16), 80)]
        for j in range(1, 8):
            rcopy(bf_recv.at[b, j], bf_recv.at[b, j], bf_s.at[b, j], bf_r.at[b, j],
                  part_dev).wait_recv()
            tot = tot + bf_recv[b, j].astype(F32)
        bx_send[b] = tot
    bx = {}
    for k in range(1, NX):
        xx = xo(k)
        bx[k] = rcopy(bx_send.at[lax.rem(xx, 2)], bx_recv.at[k - 1],
                      bx_s.at[k], bx_r.at[k], dev(xx, y, z, c))

        @pl.when(lax.div(xx, 2) == c)
        def _():
            bx[k].start()

    for cp in gz:
        cp.wait_recv()
    g_y[y] = sum8(g_z)
    gy = spread(g_y, y, gy_s, gy_r, NY, lambda k: dev(x, yo(k), z, c))

    tot = a_acc[yl, pl.ds(pl.multiple_of(yh * 80, 16), 80)]
    for j in range(1, NY):
        rcopy(ay_recv.at[j], ay_recv.at[j], ay_s.at[j], ay_r.at[j], part_dev).wait_recv()
        tot = tot + ay_recv[j].astype(F32)
    a_fin[0:80] = tot
    for i in range(NZ):
        az_send[i] = a_fin[10 * i:10 * i + 16]
    az = {}
    for k in range(1, NZ):
        zz = zo(k)
        az[k] = go(rcopy(az_send.at[zz], az_recv.at[k], az_s.at[k], az_r.at[k], dev(x, y, zz, c)))

    yd = jnp.where(odd == 1, z, y)
    slot = jnp.where(odd == 1, y, z)
    bz = {}
    for k in range(NZ):
        zz = zo(k)
        for o in range(2):
            bz[(k, o)] = rcopy(bz_send.at[zz], bz_recv.at[slot], bz_s.at[k, o], bz_r.at[slot],
                               dev(x, yd, zz, oc if o else c))

    @pl.when(mine)
    def _():
        t = bx_send[odd]
        for k in (1, 3, 2):
            bx[k].wait_recv()
            t = t + bx_recv[k - 1]
        b_fin[0:80] = t
        for i in range(NZ):
            bz_send[i] = b_fin[10 * i:10 * i + 16]

        @pl.when(yd == y)
        def _():
            bz_recv[slot] = bz_send[z]

        @pl.when(yd != y)
        def _():
            bz[(0, 0)].start()

        for k in range(NZ):
            for o in range(0 if k else 1, 2):
                bz[(k, o)].start()

    for cp in gy:
        cp.wait_recv()
    g_mine[...] = sum8(g_y)
    gf = go(rcopy(g_mine, g_full, gf_s, gf_r, part_dev))

    ta = az_send[z]
    for k in range(1, NZ):
        az[k].wait_recv()
        ta = ta + az_recv[k]
    wg_out[:, 0:128] = ta[0:10]

    for i in range(NZ):
        local = jnp.logical_and(jnp.logical_and(mine, yd == y), slot == i)

        @pl.when(jnp.logical_not(local))
        def _():
            rcopy(bz_recv.at[i], bz_recv.at[i], bz_s.at[0, 0], bz_r.at[i], part_dev).wait_recv()

    tb = sum8(bz_recv)
    tb = jnp.where(c == 0, tb, pltpu.roll(tb, 64, 1))
    wg_out[:, 128:192] = tb[0:10, 0:64]

    gf.wait_recv()

    @pl.when(c == 0)
    def _():
        gg_out[0:24] = g_mine[...]
        gg_out[24:40] = g_full[8:24]

    @pl.when(c == 1)
    def _():
        gg_out[0:16] = g_full[0:16]
        gg_out[16:40] = g_mine[...]

    for cp in started:
        cp.wait_send()
    for j in range(1, 8):
        rcopy(ay_recv.at[j], ay_recv.at[j], ay_s.at[j], ay_r.at[j], part_dev).wait_send()
        for b in range(2):
            rcopy(bf_recv.at[b, j], bf_recv.at[b, j], bf_s.at[b, j], bf_r.at[b, j],
                  part_dev).wait_send()
    for k in range(NX):
        xx = xo(k)

        @pl.when(lax.div(xx, 2) != c)
        def _():
            for l in range(2):
                bcp[(k, l)].wait_send()

        if k:
            @pl.when(lax.div(xx, 2) == c)
            def _():
                bx[k].wait_send()

    @pl.when(mine)
    def _():
        @pl.when(yd != y)
        def _():
            bz[(0, 0)].wait_send()

        for k in range(NZ):
            for o in range(0 if k else 1, 2):
                bz[(k, o)].wait_send()


def leave(wg_in, gg_in, wg_out, gg_out):
    wg_out[...] = wg_in[...]
    gg_out[...] = gg_in[...]


def on_device(hidden, targets, head_weight, norm_gain):
    dma = pltpu.SemaphoreType.DMA
    vm = pltpu.VMEM
    scratch = [
        vm((TOK, D), BF16), vm((TOK, D), BF16), vm((TOK, 128), F32),
        vm((16, 480, 128), BF16), vm((8, QW, 256), BF16),
        vm((TOK, 256), F32), vm((TOK, 256), BF16), vm((TOK, 256), BF16),
        vm((4, 2, 320, 128), F32), vm((4, 2, 320, 128), BF16), vm((4, 2, 320, 128), BF16),
        vm((4, 2, 320, 128), F32), vm((4, 2, 320, 128), BF16), vm((4, 2, 320, 128), BF16),
        vm((3, 2, 320, 128), BF16), vm((3, 2, 320, 128), BF16), vm((2, 320, 128), F32),
        vm((2, 320, 128), BF16), vm((8, 80, 128), BF16),
        vm((96, 128), F32), vm((8, 16, 128), F32), vm((8, 16, 128), F32),
        vm((2, 2, 320, 128), BF16), vm((2, 2, 320, 128), F32), vm((2, 8, 80, 128), BF16),
        vm((2, 80, 128), F32), vm((3, 80, 128), F32),
        vm((96, 128), F32), vm((8, 16, 128), F32), vm((8, 16, 128), F32),
        vm((40, 128), F32), vm((24, 128), F32), vm((4, 24, 128), F32),
        vm((8, 24, 128), F32), vm((8, 24, 128), F32), vm((24, 128), F32), vm((24, 128), F32),
        dma((4,)),
        dma((4, 2)), dma((4, 2)), dma((4, 2)), dma((4, 2)), dma((4, 2)), dma((4, 2)),
        dma((4, 2)), dma((4, 2)), dma((4, 2)), dma((4, 2)),
        dma((4, 2)), dma((4, 2)), dma((8,)), dma((8,)), dma((8,)), dma((8,)),
        dma((2, 8)), dma((2, 8)), dma((4,)), dma((4,)), dma((8, 2)), dma((8,)),
        dma, dma, dma((4,)), dma((4,)), dma((8,)), dma((8,)), dma((8,)), dma((8,)), dma, dma,
    ]
    vspec = pl.BlockSpec(memory_space=pltpu.VMEM)
    outs = (jax.ShapeDtypeStruct((10, V), F32), jax.ShapeDtypeStruct((40, 128), F32))
    wg, gg = pl.pallas_call(
        kernel,
        out_shape=outs,
        in_specs=[pl.BlockSpec(memory_space=pl.ANY), vspec, vspec, vspec],
        out_specs=(vspec, vspec),
        scratch_shapes=scratch,
        compiler_params=pltpu.CompilerParams(
            collective_id=0, has_side_effects=True, vmem_limit_bytes=56 * 1024 * 1024),
        cost_estimate=pl.CostEstimate(flops=3 * 2 * TOK * D * V, bytes_accessed=TOK * D * 2,
                                      transcendentals=TOK * V),
    )(hidden, targets, head_weight.T, norm_gain.reshape(1, D))
    wg, gg = pl.pallas_call(
        leave, out_shape=outs, in_specs=[vspec, vspec], out_specs=(vspec, vspec),
    )(wg, gg)
    return wg, gg.reshape(D)


def solution(mesh):
    placed = (P(("section", "dp"), None), P(("section", "dp")), P("section", None), P())
    return jax.shard_map(
        on_device,
        mesh=mesh,
        in_specs=placed,
        out_specs=(P(("section", "dp"), None), P()),
        check_vma=False,
    )
```

time: 68.3 us -> 62.3 us (0.912)
  the two profiles are of different devices: /device:TPU:1 before, /device:TPU:19 now
where the time goes in v2:
time: 62.3 us; the launch traced here: 62.1 us
  Pallas kernels  61.5 us (99%)
  between operations  0.64 us (1%)
    pallas_call x1, Pallas kernels, on_device(): pl.pallas_call(kernel, out_shape=outs, in_specs=[pl.BlockSpec(memory_spac...  60.1 us
    pallas_call x1, Pallas kernels, on_device(): pl.pallas_call(leave, out_shape=outs, in_specs=[vspec, vspec], out_specs=...  1.36 us

profile of v2, /device:TPU:19, one launch (start us, length us, event | category | flops | bytes accessed | tf_op | source)
XLA Modules:
  0.0 62.1 jit_solution(15234508690030274704)
XLA Ops:
  0.6 60.1 %shard_map.59 = (f32[10,192]{1,0:T(8,128)}, f32[40,128]{1,0:T(8,128)}) custom-call(bf16[384,5120]{1,0:T(8,128)(2,1)} %hid.1, s32[384]{0:T(512)} %tgt.1, bf16[192,320]{1,0:T(8,128)(2,1)} %bitcast.3, f32[1,5120]{1,0:T(1,128)} %bitcast.4), custom_call_target="tpu_custom_call" | custom-call | flops 2264924160 | bytes 3932160 | tf_op jit(solution)/shard_map/pallas_call | solution.py:494
  60.8 1.4 %shard_map.60 = (f32[10,192]{1,0:T(8,128)}, f32[40,128]{1,0:T(8,128)}) custom-call(f32[10,192]{1,0:T(8,128)} %get-tuple-element.6.wg_in, f32[40,128]{1,0:T(8,128)} %get-tuple-element.7.gg_in), custom_call_target="tpu_custom_call" | custom-call | tf_op jit(solution)/shard_map/pallas_call | solution.py:505

commit v3 on v2

v3 whole, which is shorter than its diff:
```python
import jax
import jax.numpy as jnp
from jax import lax
from jax.experimental import pallas as pl
from jax.experimental.pallas import tpu as pltpu
from jax.sharding import PartitionSpec as P

D = 5120
V = 192
TOK = 384
NX, NY, NZ = 4, 8, 8
QW = 640
MESH = pl.DeviceIdType.MESH
F32 = jnp.float32
BF16 = jnp.bfloat16
SCALE = 1.0 / TOK**0.5


def kernel(
    hid, tgt_in, wt_in, gain_in, wg_out, gg_out,
    tgt, wt, gain, h, s, wp, wu, logit, dle,
    a_keep, a_send, a_core, b_keep, b_send, b_core,
    ax_send, ax_recv, a_pend, a_acc,
    ay_send, ay_recv, a1_p32, a1_p16, a1_recv, a_fin0, a_fin1, az0_send, az1_send, az_recv,
    b0_send, b0_acc, b0_recv, b1_acc, b1_p32, b1_p16, b1_recv,
    bx_send, bx_recv, b_fin, bz_send, bz_recv,
    g_loc, g_core, g_x, g_y, g_z, g_mine, g_full,
    hsem,
    wx_s, wx_r, wy_s, wy_r, wc_s, wc_r, ac_s, ac_r, bc_s, bc_r,
    ax_s, axr_r, ax_r, ay_s, ay_r, a1_s, a1_r, az_s, az_r,
    b0_s, b0_r, b1_s, b1_r, bx_s, bx_r, bz_s, bz_r,
    gc_s, gc_r, gx_s, gx_r, gy_s, gy_r, gz_s, gz_r, gf_s, gf_r,
):
    sec = lax.axis_index("section")
    dp = lax.axis_index("dp")
    c = lax.rem(sec, 2)
    yl = lax.rem(lax.div(sec, 2), 2)
    x = lax.div(sec, 4)
    yh = lax.div(dp, NZ)
    z = lax.rem(dp, NZ)
    y = yh * 2 + yl
    oc = 1 - c
    odd = lax.rem(x, 2)
    mine = lax.div(x, 2) == c

    def dev(x_, y_, z_, c_):
        return (x_ * 4 + lax.rem(y_, 2) * 2 + c_, lax.div(y_, 2) * NZ + z_)

    def xo(k):
        return lax.rem(x + k, NX)

    def yo(k):
        return lax.rem(y + k, NY)

    def zo(k):
        return lax.rem(z + k, NZ)

    def rcopy(src, dst, ss, rs, to):
        return pltpu.make_async_remote_copy(
            src_ref=src, dst_ref=dst, send_sem=ss, recv_sem=rs,
            device_id=to, device_id_type=MESH)

    barrier = pltpu.get_barrier_semaphore()
    peers = [dev(x, y, z, oc)]
    peers += [dev(xo(k), y, z, c) for k in range(1, NX)]
    peers += [dev(x, yo(k), z, c) for k in range(1, NY)]
    peers += [dev(x, y, zo(k), c) for k in range(1, NZ)]
    for p in peers:
        pl.semaphore_signal(barrier, inc=1, device_id=p, device_id_type=MESH)

    def fetch(src, dst, i):
        cp = pltpu.make_async_copy(src, dst, hsem.at[i])
        cp.start()
        return cp

    wcopy = fetch(wt_in, wt, 4)
    hcopies = [fetch(hid.at[pl.ds(96 * i, 96)], h.at[pl.ds(96 * i, 96)], i) for i in range(4)]
    gcopy = fetch(gain_in, gain, 5)
    tcopy = fetch(tgt_in, tgt, 6)

    eye = (lax.broadcasted_iota(jnp.int32, (320, 320), 0)
           == lax.broadcasted_iota(jnp.int32, (320, 320), 1)).astype(BF16)
    wcopy.wait()
    w = lax.dot_general(eye, wt[...], (((1,), (1,)), ((), ())), preferred_element_type=F32)
    wp[sec, 0:320, :] = w[:, 0:128].astype(BF16)
    wp[sec, 320:480, :] = jnp.concatenate(
        [w[0:160, 128:192], w[160:320, 128:192]], axis=1).astype(BF16)

    pl.semaphore_wait(barrier, len(peers))

    def go(cp):
        cp.start()
        return cp

    def got(ref, rs):
        rcopy(ref, ref, gf_s, rs, dev(x, y, z, oc)).wait_recv()

    def sent(ref, ss):
        rcopy(ref, ref, ss, gf_r, dev(x, y, z, oc)).wait_send()

    def shard(k, l, cc):
        return xo(NX - k if k else 0) * 4 + l * 2 + cc

    def half(sh, i):
        return wp.at[sh, pl.ds(240 * i, 240)]

    wx, wc = {}, {}

    def send_x(k, i):
        wx[(k, i)] = go(rcopy(half(sec, i), half(sec, i), wx_s, wx_r.at[k - 1, i],
                              dev(xo(k), y, z, c)))

    def fwd_y(k, i):
        sh = shard(k, yl, c)
        go(rcopy(half(sh, i), half(sh, i), wy_s, wy_r.at[k], dev(x, yo(NY - 1 if i else 1), z, c)))

    def fwd_c(k, j):
        sh = shard(k, yl if j == 0 else 1 - yl, c)
        wc[(k, j)] = go(rcopy(wp.at[sh], wp.at[sh], wc_s, wc_r.at[k, j], dev(x, y, z, oc)))

    send_x(1, 0)
    send_x(3, 1)
    fwd_y(0, 0)
    fwd_y(0, 1)
    send_x(1, 1)
    send_x(3, 0)
    fwd_c(0, 0)

    def rows(i, carry):
        r0 = pl.multiple_of(i * 16, 16)
        acc = jnp.zeros((16, 128), F32)
        for j in range(D // 128):
            v = h[pl.ds(r0, 16), j * 128:(j + 1) * 128].astype(F32)
            acc = acc + v * v
        ms = jnp.sum(acc, axis=1, keepdims=True) * (1.0 / D)
        r = jnp.broadcast_to(lax.rsqrt(ms + 1e-05), (16, 128))
        for j in range(D // 128):
            v = h[pl.ds(r0, 16), j * 128:(j + 1) * 128].astype(F32)
            gj = gain[:, j * 128:(j + 1) * 128]
            s[pl.ds(r0, 16), j * 128:(j + 1) * 128] = ((v * r) * gj).astype(BF16)
        return carry

    def block(i):
        if i == 0:
            gcopy.wait()
        if i % 2 == 0:
            hcopies[i // 2].wait()
        lax.fori_loop(3 * i, 3 * i + 3, rows, 0)

    def take_x(k, i):
        wx[(k, i)].wait_recv()
        if (k, i) in ((1, 0), (3, 1)):
            sh = shard(k, yl, c)
            wx[(2, i)] = go(rcopy(half(sh, i), half(sh, i), wx_s, wx_r.at[1, i],
                                  dev(xo(k), y, z, c)))
        fwd_y(k, i)

    def take_y(k):
        got(wp.at[0], wy_r.at[k])
        fwd_c(k, 1)

    def unpack(k, j):
        l = yl if j == 0 else 1 - yl
        q = xo(NX - k if k else 0) * 2 + l
        for cc in range(2):
            sh = q * 2 + cc
            wu[q, cc * 320:(cc + 1) * 320, 0:128] = wp[sh, 0:320, :]
            b = wp[sh, 320:480, :]
            wu[q, cc * 320:cc * 320 + 160, 128:256] = b
            wu[q, cc * 320 + 160:(cc + 1) * 320, 128:256] = pltpu.roll(
                b.astype(F32), 64, 1).astype(BF16)
        return q

    def add_logits(k, j):
        wc[(k, j)].wait_recv()
        q = unpack(k, j)
        part = jnp.dot(s[:, pl.ds(pl.multiple_of(q * QW, 128), QW)], wu[q],
                       preferred_element_type=F32)
        if (k, j) == (0, 0):
            logit[...] = part
        else:
            logit[...] += part

    for i in range(6):
        block(i)
    take_x(1, 0)
    take_x(3, 1)
    block(6)
    block(7)
    take_x(1, 1)
    take_x(3, 0)
    fwd_c(1, 0)
    fwd_c(3, 0)
    take_y(0)
    add_logits(0, 0)
    add_logits(1, 0)
    take_x(2, 0)
    take_x(2, 1)
    fwd_c(2, 0)
    add_logits(3, 0)
    add_logits(0, 1)
    add_logits(2, 0)
    take_y(1)
    take_y(3)
    add_logits(1, 1)
    take_y(2)
    add_logits(3, 1)
    add_logits(2, 1)

    lane = lax.broadcasted_iota(jnp.int32, (TOK, 256), 1)
    tcopy.wait()
    t_col = jnp.transpose(jnp.broadcast_to(tgt[...].reshape(1, TOK).astype(F32), (128, TOK)))
    tc = jnp.concatenate([t_col, t_col], axis=1)
    onehot = (tc == lane.astype(F32)).astype(F32)
    lg = jnp.where(lane < V, logit[...], -3e38)
    m = jnp.max(lg, axis=1, keepdims=True)
    e = jnp.where(lane < V, jnp.exp(lg - m), 0.0)
    p = e / jnp.sum(e, axis=1, keepdims=True)
    dl = ((p - onehot) * SCALE).astype(BF16)
    up = dl[:, 128:256].astype(F32)
    dle[:, 0:128] = dl[:, 0:128]
    dle[:, 128:256] = (up + pltpu.roll(up, 64, 1)).astype(BF16)

    lane_lo = lax.broadcasted_iota(jnp.int32, (320, 128), 1) < 64
    pick_row = lax.broadcasted_iota(jnp.int32, (8, 128), 0)
    pick_half = (lax.broadcasted_iota(jnp.int32, (8, 128), 1) >= 64).astype(jnp.int32)
    ones = jnp.ones((8, 128), BF16)
    halves = (pick_row == pick_half).astype(BF16)
    part_dev = dev(x, y, z, oc)
    g_loc[...] = jnp.zeros((16, 320), F32)

    def chunk(l, k):
        xx = xo(k)
        q = xx * 2 + l
        wv = lax.dot_general(
            s[:, pl.ds(pl.multiple_of(q * QW, 128), QW)], dle[...],
            (((0,), (0,)), ((), ())), preferred_element_type=F32)
        top, bot = wv[0:320, 0:128], wv[320:640, 0:128]
        a_send[xx, l] = jnp.where(c == 0, bot, top).astype(BF16)
        go(rcopy(a_send.at[xx, l], a_core.at[xx, l], ac_s, ac_r.at[k, l], part_dev))
        bq = jnp.where(lane_lo, wv[0:320, 128:256], wv[320:640, 128:256])
        b_send[xx, l] = bq.astype(BF16)

        @pl.when(lax.div(xx, 2) != c)
        def _():
            go(rcopy(b_send.at[xx, l], b_core.at[xx, l], bc_s, bc_r.at[lax.rem(xx, 2), l], part_dev))

        a_keep[xx, l] = jnp.where(c == 0, top, bot)
        b_keep[xx, l] = bq

    def x_send(l, n, v):
        ax_send[l, n] = v.astype(BF16)
        rs = axr_r.at[l, n // 3] if n % 3 == 0 else ax_r.at[l]
        go(rcopy(ax_send.at[l, n], ax_recv.at[l, n], ax_s, rs, dev(xo(1 if n < 3 else 3), y, z, c)))

    def x_relay(l):
        for i in range(2):
            got(ax_recv.at[l, 3 * i], axr_r.at[l, i])
            x_send(l, 3 * i + 2, a_pend[l, i] + ax_recv[l, 3 * i].astype(F32))

    def row_sums(pick, v):
        hi = v.astype(BF16)
        lo = (v - hi.astype(F32)).astype(BF16)
        dims = (((1,), (1,)), ((), ()))
        return (lax.dot_general(pick, hi, dims, preferred_element_type=F32)
                + lax.dot_general(pick, lo, dims, preferred_element_type=F32))

    def by_z(src, dst):
        for j in range(NZ):
            for i in range(4):
                dst[j, 10 * i:10 * i + 16] = src[80 * i + 10 * j:80 * i + 10 * j + 16]

    def chip_sum(l, k):
        xx = xo(k)
        q = xx * 2 + l
        got(a_core.at[0, 0], ac_r.at[k, l])
        tot = a_keep[xx, l] + a_core[xx, l].astype(F32)
        if k == 0:
            a_acc[l, 0:320] = tot
        if k == 1:
            x_send(l, 1, tot[160:320])
            a_pend[l, 0] = tot[0:160]
        if k == 2:
            x_send(l, 0, tot[0:160])
            x_send(l, 3, tot[160:320])
        if k == 3:
            x_send(l, 4, tot[0:160])
            a_pend[l, 1] = tot[160:320]
        wa = wu[q, pl.ds(pl.multiple_of(c * 320, 16), 320), 0:128].astype(F32)
        row = c * 8 + q
        g_loc[pl.ds(row, 1), :] += row_sums(ones, tot * wa)[0:1]

        @pl.when(lax.div(xx, 2) == c)
        def _():
            b = lax.rem(xx, 2)
            got(b_core.at[0, 0], bc_r.at[b, l])
            tot = b_keep[xx, l] + b_core[xx, l].astype(F32)

            @pl.when(b == 0)
            def _():
                b0_acc[l] = tot
                b0_send[l] = tot.astype(BF16)
                for i in range(4):
                    j = lax.rem(i * 2 + l + 8 - y, 8)

                    @pl.when(j != 0)
                    def _():
                        go(rcopy(b0_send.at[l, pl.ds(80 * i, 80)], b0_recv.at[j], b0_s, b0_r,
                                 dev(x, i * 2 + l, z, c)))

            @pl.when(b == 1)
            def _():
                b1_acc[0:320] = tot
                by_z(b1_acc, b1_p32.at[l])
                b1_p16[l] = b1_p32[l].astype(BF16)
                for j in range(1, NZ):
                    go(rcopy(b1_p16.at[l, zo(j)], b1_recv.at[j, l], b1_s, b1_r, dev(x, y, zo(j), c)))

            wb = jnp.concatenate(
                [jnp.where(lane_lo[0:160], wu[q, 0:160, 128:256], wu[q, 480:640, 128:256]),
                 jnp.where(lane_lo[0:160], wu[q, 160:320, 128:256], wu[q, 320:480, 128:256])],
                axis=0).astype(F32)
            t = row_sums(halves, tot * wb)
            g_loc[pl.ds(q, 1), :] += t[0:1]
            g_loc[pl.ds(8 + q, 1), :] += t[1:2]

    a_acc[:, 320:336] = jnp.zeros((2, 16, 128), F32)
    b1_acc[320:336] = jnp.zeros((16, 128), F32)
    a1_p32[:, 40:48] = jnp.zeros((8, 8, 128), F32)
    b1_p32[:, :, 40:48] = jnp.zeros((2, 8, 8, 128), F32)
    bx_send[:, 80:96] = jnp.zeros((2, 16, 128), F32)
    a_fin0[80:96] = jnp.zeros((16, 128), F32)
    b_fin[96:112] = jnp.zeros((16, 128), F32)

    before = None
    for l in range(2):
        for k in (2, 1, 3, 0):
            chunk(l, k)
            if before:
                chip_sum(*before)
            before = (l, k)
    x_relay(0)
    chip_sum(*before)

    grow = pl.multiple_of(c * 8, 8)
    gorow = pl.multiple_of(oc * 8, 8)
    go(rcopy(g_loc.at[pl.ds(gorow, 8)], g_core, gc_s, gc_r, part_dev))
    x_relay(1)

    def spread(buf, own, ss, rs, count, to):
        for k in range(1, count):
            go(rcopy(buf.at[own], buf.at[own], ss, rs, to(k)))

    def sum8(v):
        return ((v[0] + v[1]) + (v[2] + v[3])) + ((v[4] + v[5]) + (v[6] + v[7]))

    got(g_core, gc_r)
    g_z[z] = g_loc[pl.ds(grow, 8)] + g_core[...]
    spread(g_z, z, gz_s, gz_r, NZ, lambda k: dev(x, y, zo(k), c))

    def x_done(l):
        got(ax_recv.at[l, pl.ds(0, 4)], ax_r.at[l])
        for i, (m, n) in enumerate(((4, 2), (1, 5))):
            a_acc[l, 160 * i:160 * i + 160] += ax_recv[l, m].astype(F32) + ax_recv[l, n].astype(F32)

    x_done(0)
    ay_send[...] = a_acc[0, 0:320].astype(BF16)
    for i in range(4):
        j = lax.rem(i * 2 + 8 - y, 8)

        @pl.when(j != 0)
        def _():
            go(rcopy(ay_send.at[pl.ds(80 * i, 80)], ay_recv.at[j], ay_s, ay_r, dev(x, i * 2, z, c)))

    x_done(1)
    by_z(a_acc.at[1], a1_p32)
    a1_p16[...] = a1_p32[...].astype(BF16)
    for j in range(1, NZ):
        go(rcopy(a1_p16.at[zo(j)], a1_recv.at[j], a1_s, a1_r, dev(x, y, zo(j), c)))

    got(b0_recv.at[pl.ds(1, 7)], b0_r)
    t = b0_acc[yl, pl.ds(pl.multiple_of(yh * 80, 16), 80)]
    for j in range(1, NY):
        t = t + b0_recv[j].astype(F32)
    bx_send[0, 0:80] = t
    got(b1_recv.at[pl.ds(1, 7)], b1_r)
    for l in range(2):
        t = b1_p32[l, z]
        for j in range(1, NZ):
            t = t + b1_recv[j, l].astype(F32)
        bx_send[1, 48 * l:48 * l + 48] = t
    for k in range(1, NX):
        xx = xo(k)

        @pl.when(lax.div(xx, 2) == c)
        def _():
            go(rcopy(bx_send.at[lax.rem(xx, 2)], bx_recv.at[k - 1], bx_s, bx_r, dev(xx, y, z, c)))

    got(g_z.at[pl.ds(0, 7)], gz_r)
    g_y[y] = sum8(g_z)
    spread(g_y, y, gy_s, gy_r, NY, lambda k: dev(x, yo(k), z, c))

    @pl.when(yl == 0)
    def _():
        got(ay_recv.at[pl.ds(1, 7)], ay_r)
        t = a_acc[0, pl.ds(pl.multiple_of(yh * 80, 16), 80)]
        for j in range(1, NY):
            t = t + ay_recv[j].astype(F32)
        a_fin0[0:80] = t
        for i in range(NZ):
            az0_send[i] = a_fin0[10 * i:10 * i + 16]
        az_recv[z] = az0_send[z]
        for k in range(1, NZ):
            go(rcopy(az0_send.at[zo(k)], az_recv.at[z], az_s, az_r, dev(x, y, zo(k), c)))

    got(a1_recv.at[pl.ds(1, 7)], a1_r)
    t = a1_p32[z]
    for j in range(1, NZ):
        t = t + a1_recv[j].astype(F32)
    a_fin1[...] = t
    for i in range(4):
        az1_send[i] = a_fin1[10 * i:10 * i + 16]
    for i in range(4):
        @pl.when(y != 2 * i + 1)
        def _():
            go(rcopy(az1_send.at[i], az_recv.at[y], az_s, az_r, dev(x, 2 * i + 1, z, c)))

        @pl.when(y == 2 * i + 1)
        def _():
            az_recv[y] = az1_send[i]

    slot = jnp.where(odd == 1, y, z)

    @pl.when(mine)
    def _():
        got(bx_recv, bx_r)
        b_fin[0:96] = (bx_send[odd] + bx_recv[0]) + (bx_recv[1] + bx_recv[2])

        @pl.when(odd == 0)
        def _():
            for n in range(8):
                bz_send[n] = b_fin[10 * n:10 * n + 16]

        @pl.when(odd == 1)
        def _():
            for n in range(8):
                o = (n % 2) * 48 + (n // 2) * 10
                bz_send[n] = b_fin[o:o + 16]

        bz_recv[slot] = bz_send[slot]
        for k in range(8):
            n = lax.rem(slot + k, 8)
            to_y = jnp.where(odd == 1, n, y)
            to_z = jnp.where(odd == 1, z, n)
            for o in range(0 if k else 1, 2):
                go(rcopy(bz_send.at[n], bz_recv.at[slot], bz_s, bz_r, dev(x, to_y, to_z, oc if o else c)))

    got(g_y.at[pl.ds(0, 7)], gy_r)
    g_x[x] = sum8(g_y)
    spread(g_x, x, gx_s, gx_r, NX, lambda k: dev(xo(k), y, z, c))

    got(az_recv.at[pl.ds(0, 7)], az_r)
    wg_out[:, 0:128] = sum8(az_recv)[0:10]

    @pl.when(mine)
    def _():
        got(bz_recv.at[pl.ds(0, 7)], bz_r)

    @pl.when(jnp.logical_not(mine))
    def _():
        got(bz_recv, bz_r)

    tb = sum8(bz_recv)
    tb = jnp.where(c == 0, tb, pltpu.roll(tb, 64, 1))
    wg_out[:, 128:192] = tb[0:10, 0:64]

    got(g_x.at[pl.ds(0, 3)], gx_r)
    g_mine[...] = (g_x[0] + g_x[1]) + (g_x[2] + g_x[3])
    gf = go(rcopy(g_mine, g_full, gf_s, gf_r, part_dev))
    gf.wait_recv()
    gg_out[pl.ds(grow, 8)] = g_mine[...]
    gg_out[pl.ds(gorow, 8)] = g_full[...]

    gf.wait_send()
    sent(wp.at[pl.ds(0, 3)], wx_s)
    sent(wp.at[pl.ds(0, 4)], wy_s)
    sent(wp.at[pl.ds(0, 8)], wc_s)
    sent(a_send, ac_s)
    sent(b_send.at[pl.ds(0, 2)], bc_s)
    sent(ax_send, ax_s)
    sent(g_core, gc_s)
    sent(g_z.at[pl.ds(0, 7)], gz_s)
    sent(g_y.at[pl.ds(0, 7)], gy_s)
    sent(g_x.at[pl.ds(0, 3)], gx_s)
    sent(b0_recv.at[pl.ds(1, 7)], b0_s)
    sent(b1_recv.at[pl.ds(1, 7)], b1_s)
    sent(a1_recv.at[pl.ds(1, 7)], a1_s)

    @pl.when(yl == 0)
    def _():
        sent(ay_recv.at[pl.ds(0, 3)], ay_s)
        sent(az_recv.at[pl.ds(0, 7)], az_s)
        sent(az_recv.at[pl.ds(0, 4)], az_s)

    @pl.when(yl == 1)
    def _():
        sent(ay_recv.at[pl.ds(0, 4)], ay_s)
        sent(az_recv.at[pl.ds(0, 3)], az_s)

    @pl.when(mine)
    def _():
        sent(bx_recv.at[0], bx_s)
        sent(bz_recv, bz_s)
        sent(bz_recv.at[pl.ds(0, 7)], bz_s)

    @pl.when(jnp.logical_not(mine))
    def _():
        sent(bx_recv.at[pl.ds(0, 2)], bx_s)


def leave(wg_in, gg_in, gain, wg_out, gg_out):
    wg_out[...] = wg_in[...]
    both = jnp.concatenate([gg_in[0:8], gg_in[8:16]], axis=1)
    for q in range(8):
        for i in range(5):
            r = q * 5 + i
            gg_out[r:r + 1] = both[q:q + 1, 128 * i:128 * i + 128] / gain[r:r + 1]


def on_device(hidden, targets, head_weight, norm_gain):
    dma = pltpu.SemaphoreType.DMA
    vm = pltpu.VMEM
    scratch = [
        vm((TOK,), jnp.int32), vm((192, 320), BF16), vm((1, D), F32),
        vm((TOK, D), BF16), vm((TOK, D), BF16),
        vm((16, 480, 128), BF16), vm((8, QW, 256), BF16), vm((TOK, 256), F32), vm((TOK, 256), BF16),
        vm((4, 2, 320, 128), F32), vm((4, 2, 320, 128), BF16), vm((4, 2, 320, 128), BF16),
        vm((4, 2, 320, 128), F32), vm((4, 2, 320, 128), BF16), vm((4, 2, 320, 128), BF16),
        vm((2, 6, 160, 128), BF16), vm((2, 6, 160, 128), BF16), vm((2, 2, 160, 128), F32),
        vm((2, 336, 128), F32),
        vm((320, 128), BF16), vm((8, 80, 128), BF16),
        vm((8, 48, 128), F32), vm((8, 48, 128), BF16), vm((8, 48, 128), BF16),
        vm((96, 128), F32), vm((48, 128), F32),
        vm((8, 16, 128), F32), vm((4, 16, 128), F32), vm((8, 16, 128), F32),
        vm((2, 320, 128), BF16), vm((2, 320, 128), F32), vm((8, 80, 128), BF16),
        vm((336, 128), F32), vm((2, 8, 48, 128), F32), vm((2, 8, 48, 128), BF16), vm((8, 2, 48, 128), BF16),
        vm((2, 96, 128), F32), vm((3, 96, 128), F32),
        vm((112, 128), F32), vm((8, 16, 128), F32), vm((8, 16, 128), F32),
        vm((16, 320), F32), vm((8, 320), F32), vm((4, 8, 320), F32),
        vm((8, 8, 320), F32), vm((8, 8, 320), F32), vm((8, 320), F32), vm((8, 320), F32),
        dma((7,)),
        dma, dma((3, 2)), dma, dma((4,)), dma, dma((4, 2)), dma, dma((4, 2)), dma, dma((2, 2)),
        dma, dma((2, 2)), dma((2,)), dma, dma, dma, dma, dma, dma,
        dma, dma, dma, dma, dma, dma, dma, dma,
        dma, dma, dma, dma, dma, dma, dma, dma, dma, dma,
    ]
    vspec = pl.BlockSpec(memory_space=pltpu.VMEM)
    wg, gg = pl.pallas_call(
        kernel,
        out_shape=(jax.ShapeDtypeStruct((10, V), F32), jax.ShapeDtypeStruct((16, 320), F32)),
        in_specs=[pl.BlockSpec(memory_space=pl.ANY)] * 4,
        out_specs=(vspec, vspec),
        scratch_shapes=scratch,
        compiler_params=pltpu.CompilerParams(
            collective_id=0, has_side_effects=True, vmem_limit_bytes=56 * 1024 * 1024),
        cost_estimate=pl.CostEstimate(flops=3 * 2 * TOK * D * V, bytes_accessed=TOK * D * 2,
                                      transcendentals=TOK * V),
    )(hidden, targets, head_weight.T, norm_gain.reshape(1, D))
    wg, gg = pl.pallas_call(
        leave,
        out_shape=(jax.ShapeDtypeStruct((10, V), F32), jax.ShapeDtypeStruct((40, 128), F32)),
        in_specs=[vspec] * 3,
        out_specs=(vspec, vspec),
    )(wg, gg, norm_gain.reshape(40, 128))
    return wg, gg.reshape(D)


def solution(mesh):
    placed = (P(("section", "dp"), None), P(("section", "dp")), P("section", None), P())
    return jax.shard_map(
        on_device,
        mesh=mesh,
        in_specs=placed,
        out_specs=(P(("section", "dp"), None), P()),
        check_vma=False,
    )
```

time: 62.3 us -> 56.7 us (0.910)
  the two profiles are of different devices: /device:TPU:19 before, /device:TPU:1 now
where the time goes in v3:
time: 56.7 us; the launch traced here: 56.6 us
  Pallas kernels  55.9 us (99%)
  between operations  0.64 us (1%)
    pallas_call x1, Pallas kernels, on_device(): pl.pallas_call(kernel, out_shape=(jax.ShapeDtypeStruct((10, V), F32), jax...  54.5 us
    pallas_call x1, Pallas kernels, on_device(): pl.pallas_call(leave, out_shape=(jax.ShapeDtypeStruct((10, V), F32), jax....  1.45 us

profile of v3, /device:TPU:1, one launch (start us, length us, event | category | flops | bytes accessed | tf_op | source)
XLA Modules:
  0.0 56.6 jit_solution(8458654762356984308)
XLA Ops:
  0.6 54.5 %shard_map.59 = (f32[10,192]{1,0:T(8,128)}, f32[16,320]{1,0:T(8,128)}) custom-call(bf16[384,5120]{1,0:T(8,128)(2,1)} %hid.1, s32[384]{0:T(512)} %tgt_in.1, bf16[192,320]{1,0:T(8,128)(2,1)} %bitcast.6, f32[1,5120]{1,0:T(1,128)} %bitcast.4), custom_call_target="tpu_custom_call" | custom-call | flops 2264924160 | bytes 3932160 | tf_op jit(solution)/shard_map/pallas_call | solution.py:558
  55.1 1.4 %shard_map.60 = (f32[10,192]{1,0:T(8,128)}, f32[40,128]{1,0:T(8,128)}) custom-call(f32[10,192]{1,0:T(8,128)} %get-tuple-element.6.wg_in, f32[16,320]{1,0:T(8,128)} %get-tuple-element.7.gg_in, f32[40,128]{1,0:T(8,128)} %bitcast.5), custom_call_target="tpu_custom_call" | custom-call | tf_op jit(solution)/shard_map/pallas_call | solution.py:569

commit v4 on v3

--- a/solution.py
+++ b/solution.py
@@ -19,17 +19,17 @@
 def kernel(
     hid, tgt_in, wt_in, gain_in, wg_out, gg_out,
     tgt, wt, gain, h, s, wp, wu, logit, dle,
-    a_keep, a_send, a_core, b_keep, b_send, b_core,
+    terms, a_send, a_core, a_tot, b_send, b_core, b_tot,
     ax_send, ax_recv, a_pend, a_acc,
     ay_send, ay_recv, a1_p32, a1_p16, a1_recv, a_fin0, a_fin1, az0_send, az1_send, az_recv,
-    b0_send, b0_acc, b0_recv, b1_acc, b1_p32, b1_p16, b1_recv,
-    bx_send, bx_recv, b_fin, bz_send, bz_recv,
-    g_loc, g_core, g_x, g_y, g_z, g_mine, g_full,
+    b0_send, b0_recv, b1_p32, b1_p16, b1_recv,
+    bx_own, bx_send, bx_recv, b_fin, bz_send, bz_recv,
+    g_loc, g_core, g_x, g_y, g_z,
     hsem,
     wx_s, wx_r, wy_s, wy_r, wc_s, wc_r, ac_s, ac_r, bc_s, bc_r,
     ax_s, axr_r, ax_r, ay_s, ay_r, a1_s, a1_r, az_s, az_r,
     b0_s, b0_r, b1_s, b1_r, bx_s, bx_r, bz_s, bz_r,
-    gc_s, gc_r, gx_s, gx_r, gy_s, gy_r, gz_s, gz_r, gf_s, gf_r,
+    gc_s, gc_r, gx_s, gx_r, gy_s, gy_r, gz_s, gz_r,
 ):
     sec = lax.axis_index("section")
     dp = lax.axis_index("dp")
@@ -93,37 +93,35 @@
         return cp
 
     def got(ref, rs):
-        rcopy(ref, ref, gf_s, rs, dev(x, y, z, oc)).wait_recv()
+        rcopy(ref, ref, wx_s, rs, dev(x, y, z, oc)).wait_recv()
 
     def sent(ref, ss):
-        rcopy(ref, ref, ss, gf_r, dev(x, y, z, oc)).wait_send()
+        rcopy(ref, ref, ss, gc_r, dev(x, y, z, oc)).wait_send()
 
     def shard(k, l, cc):
         return xo(NX - k if k else 0) * 4 + l * 2 + cc
 
-    def half(sh, i):
-        return wp.at[sh, pl.ds(240 * i, 240)]
+    def piece(sh, i):
+        return wp.at[sh, pl.ds((0, 128, 240, 368)[i], (128, 112)[i % 2])]
 
     wx, wc = {}, {}
 
     def send_x(k, i):
-        wx[(k, i)] = go(rcopy(half(sec, i), half(sec, i), wx_s, wx_r.at[k - 1, i],
+        wx[(k, i)] = go(rcopy(piece(sec, i), piece(sec, i), wx_s, wx_r.at[k - 1, i],
                               dev(xo(k), y, z, c)))
 
     def fwd_y(k, i):
         sh = shard(k, yl, c)
-        go(rcopy(half(sh, i), half(sh, i), wy_s, wy_r.at[k], dev(x, yo(NY - 1 if i else 1), z, c)))
+        go(rcopy(piece(sh, i), piece(sh, i), wy_s, wy_r.at[k], dev(x, yo(1 if i < 2 else NY - 1), z, c)))
 
     def fwd_c(k, j):
         sh = shard(k, yl if j == 0 else 1 - yl, c)
         wc[(k, j)] = go(rcopy(wp.at[sh], wp.at[sh], wc_s, wc_r.at[k, j], dev(x, y, z, oc)))
 
-    send_x(1, 0)
-    send_x(3, 1)
-    fwd_y(0, 0)
-    fwd_y(0, 1)
-    send_x(1, 1)
-    send_x(3, 0)
+    for i in range(4):
+        send_x(1, i)
+        send_x(3, (i + 2) % 4)
+        fwd_y(0, (i // 2) + 2 * (i % 2))
     fwd_c(0, 0)
 
     def rows(i, carry):
@@ -149,9 +147,9 @@
 
     def take_x(k, i):
         wx[(k, i)].wait_recv()
-        if (k, i) in ((1, 0), (3, 1)):
+        if k == (1 if i < 2 else 3):
             sh = shard(k, yl, c)
-            wx[(2, i)] = go(rcopy(half(sh, i), half(sh, i), wx_s, wx_r.at[1, i],
+            wx[(2, i)] = go(rcopy(piece(sh, i), piece(sh, i), wx_s, wx_r.at[1, i],
                                   dev(xo(k), y, z, c)))
         fwd_y(k, i)
 
@@ -181,21 +179,22 @@
         else:
             logit[...] += part
 
-    for i in range(6):
+    for i in range(5):
         block(i)
-    take_x(1, 0)
-    take_x(3, 1)
-    block(6)
-    block(7)
-    take_x(1, 1)
-    take_x(3, 0)
+    for i in range(4):
+        take_x(1, i)
+        take_x(3, (i + 2) % 4)
+        if i < 3:
+            block(5 + i)
     fwd_c(1, 0)
     fwd_c(3, 0)
     take_y(0)
     add_logits(0, 0)
+    take_x(2, 0)
+    take_x(2, 2)
     add_logits(1, 0)
-    take_x(2, 0)
     take_x(2, 1)
+    take_x(2, 3)
     fwd_c(2, 0)
     add_logits(3, 0)
     add_logits(0, 1)
@@ -229,34 +228,18 @@
     part_dev = dev(x, y, z, oc)
     g_loc[...] = jnp.zeros((16, 320), F32)
 
-    def chunk(l, k):
-        xx = xo(k)
-        q = xx * 2 + l
-        wv = lax.dot_general(
-            s[:, pl.ds(pl.multiple_of(q * QW, 128), QW)], dle[...],
-            (((0,), (0,)), ((), ())), preferred_element_type=F32)
-        top, bot = wv[0:320, 0:128], wv[320:640, 0:128]
-        a_send[xx, l] = jnp.where(c == 0, bot, top).astype(BF16)
-        go(rcopy(a_send.at[xx, l], a_core.at[xx, l], ac_s, ac_r.at[k, l], part_dev))
-        bq = jnp.where(lane_lo, wv[0:320, 128:256], wv[320:640, 128:256])
-        b_send[xx, l] = bq.astype(BF16)
-
-        @pl.when(lax.div(xx, 2) != c)
-        def _():
-            go(rcopy(b_send.at[xx, l], b_core.at[xx, l], bc_s, bc_r.at[lax.rem(xx, 2), l], part_dev))
-
-        a_keep[xx, l] = jnp.where(c == 0, top, bot)
-        b_keep[xx, l] = bq
-
-    def x_send(l, n, v):
-        ax_send[l, n] = v.astype(BF16)
+    def packed(n):
+        return jnp.where(lane_lo, terms[n, 0:320, 128:256], terms[n, 320:640, 128:256])
+
+    def x_go(l, n):
         rs = axr_r.at[l, n // 3] if n % 3 == 0 else ax_r.at[l]
         go(rcopy(ax_send.at[l, n], ax_recv.at[l, n], ax_s, rs, dev(xo(1 if n < 3 else 3), y, z, c)))
 
     def x_relay(l):
         for i in range(2):
             got(ax_recv.at[l, 3 * i], axr_r.at[l, i])
-            x_send(l, 3 * i + 2, a_pend[l, i] + ax_recv[l, 3 * i].astype(F32))
+            ax_send[l, 3 * i + 2] = (a_pend[l, i] + ax_recv[l, 3 * i].astype(F32)).astype(BF16)
+            x_go(l, 3 * i + 2)
 
     def row_sums(pick, v):
         hi = v.astype(BF16)
@@ -270,82 +253,120 @@
             for i in range(4):
                 dst[j, 10 * i:10 * i + 16] = src[80 * i + 10 * j:80 * i + 10 * j + 16]
 
-    def chip_sum(l, k):
-        xx = xo(k)
-        q = xx * 2 + l
-        got(a_core.at[0, 0], ac_r.at[k, l])
-        tot = a_keep[xx, l] + a_core[xx, l].astype(F32)
-        if k == 0:
-            a_acc[l, 0:320] = tot
-        if k == 1:
-            x_send(l, 1, tot[160:320])
-            a_pend[l, 0] = tot[0:160]
-        if k == 2:
-            x_send(l, 0, tot[0:160])
-            x_send(l, 3, tot[160:320])
-        if k == 3:
-            x_send(l, 4, tot[0:160])
-            a_pend[l, 1] = tot[160:320]
+    def gain_a(n):
+        l, k = todo[n]
+        q = xo(k) * 2 + l
         wa = wu[q, pl.ds(pl.multiple_of(c * 320, 16), 320), 0:128].astype(F32)
         row = c * 8 + q
-        g_loc[pl.ds(row, 1), :] += row_sums(ones, tot * wa)[0:1]
-
-        @pl.when(lax.div(xx, 2) == c)
-        def _():
+        g_loc[pl.ds(row, 1), :] += row_sums(ones, a_tot[n] * wa)[0:1]
+
+    def gain_b(l, b):
+        q = (c * 2 + b) * 2 + l
+        wb = jnp.concatenate(
+            [jnp.where(lane_lo[0:160], wu[q, 0:160, 128:256], wu[q, 480:640, 128:256]),
+             jnp.where(lane_lo[0:160], wu[q, 160:320, 128:256], wu[q, 320:480, 128:256])],
+            axis=0).astype(F32)
+        t = row_sums(halves, b_tot[l * 4 + place(b), 0:320] * wb)
+        g_loc[pl.ds(q, 1), :] += t[0:1]
+        g_loc[pl.ds(8 + q, 1), :] += t[1:2]
+
+    todo = [(l, k) for l in range(2) for k in (2, 1, 3, 0)]
+
+    def place(b):
+        k = lax.rem(c * 2 + b + NX - x, NX)
+        return jnp.where(k == 0, 3, jnp.where(k == 3, 2, jnp.where(k == 2, 0, 1)))
+
+    def step(n):
+        r, m = n - 1, n - 3
+        if 0 <= m:
+            l, k = todo[m]
+            xx = xo(k)
+            own = lax.div(xx, 2) == c
             b = lax.rem(xx, 2)
-            got(b_core.at[0, 0], bc_r.at[b, l])
-            tot = b_keep[xx, l] + b_core[xx, l].astype(F32)
-
-            @pl.when(b == 0)
+            got(a_core.at[0], ac_r.at[m])
+
+            @pl.when(own)
             def _():
-                b0_acc[l] = tot
-                b0_send[l] = tot.astype(BF16)
+                got(b_core.at[0], bc_r.at[m])
+
+        if n < 8:
+            q = xo(todo[n][1]) * 2 + todo[n][0]
+            terms[n] = lax.dot_general(
+                s[:, pl.ds(pl.multiple_of(q * QW, 128), QW)], dle[...],
+                (((0,), (0,)), ((), ())), preferred_element_type=F32)
+        if 0 <= r < 8:
+            a_send[r] = terms[r, pl.ds(pl.multiple_of(oc * 320, 16), 320), 0:128].astype(BF16)
+            b_send[r] = packed(r).astype(BF16)
+        if 0 <= m:
+            tot = (terms[m, pl.ds(pl.multiple_of(c * 320, 16), 320), 0:128]
+                   + a_core[m].astype(F32))
+            a_tot[m] = tot
+            if k == 0:
+                a_acc[l, 0:320] = tot
+            if k == 1:
+                ax_send[l, 1] = tot[160:320].astype(BF16)
+                a_pend[l, 0] = tot[0:160]
+            if k == 2:
+                ax_send[l, 0] = tot[0:160].astype(BF16)
+                ax_send[l, 3] = tot[160:320].astype(BF16)
+            if k == 3:
+                ax_send[l, 4] = tot[0:160].astype(BF16)
+                a_pend[l, 1] = tot[160:320]
+            tot = packed(m) + b_core[m].astype(F32)
+            b_tot[m, 0:320] = tot
+            b0_send[m] = tot.astype(BF16)
+        if 0 <= r < 8:
+            go(rcopy(a_send.at[r], a_core.at[r], ac_s, ac_r.at[r], part_dev))
+
+            @pl.when(lax.div(xo(todo[r][1]), 2) != c)
+            def _():
+                go(rcopy(b_send.at[r], b_core.at[r], bc_s, bc_r.at[r], part_dev))
+
+        if 0 <= m:
+            for i in {0: (), 1: (1,), 2: (0, 3), 3: (4,)}[k]:
+                x_go(l, i)
+
+            @pl.when(jnp.logical_and(own, b == 0))
+            def _():
                 for i in range(4):
                     j = lax.rem(i * 2 + l + 8 - y, 8)
 
                     @pl.when(j != 0)
                     def _():
-                        go(rcopy(b0_send.at[l, pl.ds(80 * i, 80)], b0_recv.at[j], b0_s, b0_r,
+                        go(rcopy(b0_send.at[m, pl.ds(80 * i, 80)], b0_recv.at[j], b0_s, b0_r,
                                  dev(x, i * 2 + l, z, c)))
 
-            @pl.when(b == 1)
+            @pl.when(jnp.logical_and(own, b == 1))
             def _():
-                b1_acc[0:320] = tot
-                by_z(b1_acc, b1_p32.at[l])
+                by_z(b_tot.at[m], b1_p32.at[l])
                 b1_p16[l] = b1_p32[l].astype(BF16)
                 for j in range(1, NZ):
                     go(rcopy(b1_p16.at[l, zo(j)], b1_recv.at[j, l], b1_s, b1_r, dev(x, y, zo(j), c)))
 
-            wb = jnp.concatenate(
-                [jnp.where(lane_lo[0:160], wu[q, 0:160, 128:256], wu[q, 480:640, 128:256]),
-                 jnp.where(lane_lo[0:160], wu[q, 160:320, 128:256], wu[q, 320:480, 128:256])],
-                axis=0).astype(F32)
-            t = row_sums(halves, tot * wb)
-            g_loc[pl.ds(q, 1), :] += t[0:1]
-            g_loc[pl.ds(8 + q, 1), :] += t[1:2]
-
     a_acc[:, 320:336] = jnp.zeros((2, 16, 128), F32)
-    b1_acc[320:336] = jnp.zeros((16, 128), F32)
+    b_tot[:, 320:336] = jnp.zeros((8, 16, 128), F32)
     a1_p32[:, 40:48] = jnp.zeros((8, 8, 128), F32)
     b1_p32[:, :, 40:48] = jnp.zeros((2, 8, 8, 128), F32)
-    bx_send[:, 80:96] = jnp.zeros((2, 16, 128), F32)
+    bx_own[:, 80:96] = jnp.zeros((2, 16, 128), F32)
     a_fin0[80:96] = jnp.zeros((16, 128), F32)
     b_fin[96:112] = jnp.zeros((16, 128), F32)
 
-    before = None
+    for n in range(11):
+        step(n)
+        if n >= 8:
+            gain_a(n - 8)
+    x_relay(0)
+    for n in range(3, 8):
+        gain_a(n)
+        if n == 5:
+            x_relay(1)
     for l in range(2):
-        for k in (2, 1, 3, 0):
-            chunk(l, k)
-            if before:
-                chip_sum(*before)
-            before = (l, k)
-    x_relay(0)
-    chip_sum(*before)
+        for b in range(2):
+            gain_b(l, b)
 
     grow = pl.multiple_of(c * 8, 8)
     gorow = pl.multiple_of(oc * 8, 8)
     go(rcopy(g_loc.at[pl.ds(gorow, 8)], g_core, gc_s, gc_r, part_dev))
-    x_relay(1)
 
     def spread(buf, own, ss, rs, count, to):
         for k in range(1, count):
@@ -379,16 +400,17 @@
         go(rcopy(a1_p16.at[zo(j)], a1_recv.at[j], a1_s, a1_r, dev(x, y, zo(j), c)))
 
     got(b0_recv.at[pl.ds(1, 7)], b0_r)
-    t = b0_acc[yl, pl.ds(pl.multiple_of(yh * 80, 16), 80)]
+    t = b_tot[yl * 4 + place(0), pl.ds(pl.multiple_of(yh * 80, 16), 80)]
     for j in range(1, NY):
         t = t + b0_recv[j].astype(F32)
-    bx_send[0, 0:80] = t
+    bx_own[0, 0:80] = t
     got(b1_recv.at[pl.ds(1, 7)], b1_r)
     for l in range(2):
         t = b1_p32[l, z]
         for j in range(1, NZ):
             t = t + b1_recv[j, l].astype(F32)
-        bx_send[1, 48 * l:48 * l + 48] = t
+        bx_own[1, 48 * l:48 * l + 48] = t
+    bx_send[...] = bx_own[...].astype(BF16)
     for k in range(1, NX):
         xx = xo(k)
 
@@ -434,7 +456,8 @@
     @pl.when(mine)
     def _():
         got(bx_recv, bx_r)
-        b_fin[0:96] = (bx_send[odd] + bx_recv[0]) + (bx_recv[1] + bx_recv[2])
+        v = bx_recv[...].astype(F32)
+        b_fin[0:96] = (bx_own[odd] + v[0]) + (v[1] + v[2])
 
         @pl.when(odd == 0)
         def _():
@@ -456,8 +479,12 @@
                 go(rcopy(bz_send.at[n], bz_recv.at[slot], bz_s, bz_r, dev(x, to_y, to_z, oc if o else c)))
 
     got(g_y.at[pl.ds(0, 7)], gy_r)
-    g_x[x] = sum8(g_y)
-    spread(g_x, x, gx_s, gx_r, NX, lambda k: dev(xo(k), y, z, c))
+    g_x[c, x] = sum8(g_y)
+    mine_x = g_x.at[c, x]
+    for k in range(1, NX):
+        go(rcopy(mine_x, mine_x, gx_s, gx_r, dev(xo(k), y, z, c)))
+    for k in range(NX):
+        go(rcopy(mine_x, mine_x, gx_s, gx_r, dev(xo(k), y, z, oc)))
 
     got(az_recv.at[pl.ds(0, 7)], az_r)
     wg_out[:, 0:128] = sum8(az_recv)[0:10]
@@ -474,24 +501,20 @@
     tb = jnp.where(c == 0, tb, pltpu.roll(tb, 64, 1))
     wg_out[:, 128:192] = tb[0:10, 0:64]
 
-    got(g_x.at[pl.ds(0, 3)], gx_r)
-    g_mine[...] = (g_x[0] + g_x[1]) + (g_x[2] + g_x[3])
-    gf = go(rcopy(g_mine, g_full, gf_s, gf_r, part_dev))
-    gf.wait_recv()
-    gg_out[pl.ds(grow, 8)] = g_mine[...]
-    gg_out[pl.ds(gorow, 8)] = g_full[...]
-
-    gf.wait_send()
+    got(g_z.at[pl.ds(0, 7)], gx_r)
+    for i in range(2):
+        gg_out[8 * i:8 * i + 8] = (g_x[i, 0] + g_x[i, 1]) + (g_x[i, 2] + g_x[i, 3])
+
     sent(wp.at[pl.ds(0, 3)], wx_s)
     sent(wp.at[pl.ds(0, 4)], wy_s)
     sent(wp.at[pl.ds(0, 8)], wc_s)
     sent(a_send, ac_s)
-    sent(b_send.at[pl.ds(0, 2)], bc_s)
+    sent(b_send.at[pl.ds(0, 4)], bc_s)
     sent(ax_send, ax_s)
     sent(g_core, gc_s)
     sent(g_z.at[pl.ds(0, 7)], gz_s)
     sent(g_y.at[pl.ds(0, 7)], gy_s)
-    sent(g_x.at[pl.ds(0, 3)], gx_s)
+    sent(g_z.at[pl.ds(0, 7)], gx_s)
     sent(b0_recv.at[pl.ds(1, 7)], b0_s)
     sent(b1_recv.at[pl.ds(1, 7)], b1_s)
     sent(a1_recv.at[pl.ds(1, 7)], a1_s)
@@ -534,25 +557,26 @@
         vm((TOK,), jnp.int32), vm((192, 320), BF16), vm((1, D), F32),
         vm((TOK, D), BF16), vm((TOK, D), BF16),
         vm((16, 480, 128), BF16), vm((8, QW, 256), BF16), vm((TOK, 256), F32), vm((TOK, 256), BF16),
-        vm((4, 2, 320, 128), F32), vm((4, 2, 320, 128), BF16), vm((4, 2, 320, 128), BF16),
-        vm((4, 2, 320, 128), F32), vm((4, 2, 320, 128), BF16), vm((4, 2, 320, 128), BF16),
+        vm((8, QW, 256), F32), vm((8, 320, 128), BF16), vm((8, 320, 128), BF16),
+        vm((8, 320, 128), F32), vm((8, 320, 128), BF16), vm((8, 320, 128), BF16),
+        vm((8, 336, 128), F32),
         vm((2, 6, 160, 128), BF16), vm((2, 6, 160, 128), BF16), vm((2, 2, 160, 128), F32),
         vm((2, 336, 128), F32),
         vm((320, 128), BF16), vm((8, 80, 128), BF16),
         vm((8, 48, 128), F32), vm((8, 48, 128), BF16), vm((8, 48, 128), BF16),
         vm((96, 128), F32), vm((48, 128), F32),
         vm((8, 16, 128), F32), vm((4, 16, 128), F32), vm((8, 16, 128), F32),
-        vm((2, 320, 128), BF16), vm((2, 320, 128), F32), vm((8, 80, 128), BF16),
-        vm((336, 128), F32), vm((2, 8, 48, 128), F32), vm((2, 8, 48, 128), BF16), vm((8, 2, 48, 128), BF16),
-        vm((2, 96, 128), F32), vm((3, 96, 128), F32),
+        vm((8, 320, 128), BF16), vm((8, 80, 128), BF16),
+        vm((2, 8, 48, 128), F32), vm((2, 8, 48, 128), BF16), vm((8, 2, 48, 128), BF16),
+        vm((2, 96, 128), F32), vm((2, 96, 128), BF16), vm((3, 96, 128), BF16),
         vm((112, 128), F32), vm((8, 16, 128), F32), vm((8, 16, 128), F32),
-        vm((16, 320), F32), vm((8, 320), F32), vm((4, 8, 320), F32),
-        vm((8, 8, 320), F32), vm((8, 8, 320), F32), vm((8, 320), F32), vm((8, 320), F32),
+        vm((16, 320), F32), vm((8, 320), F32), vm((2, 4, 8, 320), F32),
+        vm((8, 8, 320), F32), vm((8, 8, 320), F32),
         dma((7,)),
-        dma, dma((3, 2)), dma, dma((4,)), dma, dma((4, 2)), dma, dma((4, 2)), dma, dma((2, 2)),
+        dma, dma((3, 4)), dma, dma((4,)), dma, dma((4, 2)), dma, dma((8,)), dma, dma((8,)),
         dma, dma((2, 2)), dma((2,)), dma, dma, dma, dma, dma, dma,
         dma, dma, dma, dma, dma, dma, dma, dma,
-        dma, dma, dma, dma, dma, dma, dma, dma, dma, dma,
+        dma, dma, dma, dma, dma, dma, dma, dma,
     ]
     vspec = pl.BlockSpec(memory_space=pltpu.VMEM)
     wg, gg = pl.pallas_call(

time: 56.7 us -> 56.3 us (level)
  no operation moved by 1% of the time
where the time goes in v4:
time: 56.3 us; the launch traced here: 56.1 us
  Pallas kernels  55.5 us (99%)
  between operations  0.64 us (1%)
    pallas_call x1, Pallas kernels, on_device(): pl.pallas_call(kernel, out_shape=(jax.ShapeDtypeStruct((10, V), F32), jax...  54 us
    pallas_call x1, Pallas kernels, on_device(): pl.pallas_call(leave, out_shape=(jax.ShapeDtypeStruct((10, V), F32), jax....  1.45 us

profile of v4, /device:TPU:1, one launch (start us, length us, event | category | flops | bytes accessed | tf_op | source)
XLA Modules:
  0.0 56.1 jit_solution(18155792510632375224)
XLA Ops:
  0.6 54.0 %shard_map.59 = (f32[10,192]{1,0:T(8,128)}, f32[16,320]{1,0:T(8,128)}) custom-call(bf16[384,5120]{1,0:T(8,128)(2,1)} %hid.1, s32[384]{0:T(512)} %tgt_in.1, bf16[192,320]{1,0:T(8,128)(2,1)} %bitcast.6, f32[1,5120]{1,0:T(1,128)} %bitcast.4), custom_call_target="tpu_custom_call" | custom-call | flops 2264924160 | bytes 3932160 | tf_op jit(solution)/shard_map/pallas_call | solution.py:582
  54.6 1.4 %shard_map.60 = (f32[10,192]{1,0:T(8,128)}, f32[40,128]{1,0:T(8,128)}) custom-call(f32[10,192]{1,0:T(8,128)} %get-tuple-element.6.wg_in, f32[16,320]{1,0:T(8,128)} %get-tuple-element.7.gg_in, f32[40,128]{1,0:T(8,128)} %bitcast.5), custom_call_target="tpu_custom_call" | custom-call | tf_op jit(solution)/shard_map/pallas_call | solution.py:593

commit v5 on v4

--- a/solution.py
+++ b/solution.py
@@ -462,13 +462,13 @@
         @pl.when(odd == 0)
         def _():
             for n in range(8):
-                bz_send[n] = b_fin[10 * n:10 * n + 16]
+                bz_send[n] = b_fin[10 * n:10 * n + 16].astype(BF16)
 
         @pl.when(odd == 1)
         def _():
             for n in range(8):
                 o = (n % 2) * 48 + (n // 2) * 10
-                bz_send[n] = b_fin[o:o + 16]
+                bz_send[n] = b_fin[o:o + 16].astype(BF16)
 
         bz_recv[slot] = bz_send[slot]
         for k in range(8):
@@ -497,7 +497,7 @@
     def _():
         got(bz_recv, bz_r)
 
-    tb = sum8(bz_recv)
+    tb = sum8(bz_recv[...].astype(F32))
     tb = jnp.where(c == 0, tb, pltpu.roll(tb, 64, 1))
     wg_out[:, 128:192] = tb[0:10, 0:64]
 
@@ -569,7 +569,7 @@
         vm((8, 320, 128), BF16), vm((8, 80, 128), BF16),
         vm((2, 8, 48, 128), F32), vm((2, 8, 48, 128), BF16), vm((8, 2, 48, 128), BF16),
         vm((2, 96, 128), F32), vm((2, 96, 128), BF16), vm((3, 96, 128), BF16),
-        vm((112, 128), F32), vm((8, 16, 128), F32), vm((8, 16, 128), F32),
+        vm((112, 128), F32), vm((8, 16, 128), BF16), vm((8, 16, 128), BF16),
         vm((16, 320), F32), vm((8, 320), F32), vm((2, 4, 8, 320), F32),
         vm((8, 8, 320), F32), vm((8, 8, 320), F32),
         dma((7,)),

time: 56.3 us -> 56.3 us (level)
  no operation moved by 1% of the time
where the time goes in v5:
time: 56.3 us; the launch traced here: 56.1 us
  Pallas kernels  55.5 us (99%)
  between operations  0.64 us (1%)
    pallas_call x1, Pallas kernels, on_device(): pl.pallas_call(kernel, out_shape=(jax.ShapeDtypeStruct((10, V), F32), jax...  54 us
    pallas_call x1, Pallas kernels, on_device(): pl.pallas_call(leave, out_shape=(jax.ShapeDtypeStruct((10, V), F32), jax....  1.45 us

profile of v5, /device:TPU:1, one launch (start us, length us, event | category | flops | bytes accessed | tf_op | source)
XLA Modules:
  0.0 56.1 jit_solution(132844960508896922)
XLA Ops:
  0.6 54.0 %shard_map.59 = (f32[10,192]{1,0:T(8,128)}, f32[16,320]{1,0:T(8,128)}) custom-call(bf16[384,5120]{1,0:T(8,128)(2,1)} %hid.1, s32[384]{0:T(512)} %tgt_in.1, bf16[192,320]{1,0:T(8,128)(2,1)} %bitcast.6, f32[1,5120]{1,0:T(1,128)} %bitcast.4), custom_call_target="tpu_custom_call" | custom-call | flops 2264924160 | bytes 3932160 | tf_op jit(solution)/shard_map/pallas_call | solution.py:582
  54.6 1.4 %shard_map.60 = (f32[10,192]{1,0:T(8,128)}, f32[40,128]{1,0:T(8,128)}) custom-call(f32[10,192]{1,0:T(8,128)} %get-tuple-element.6.wg_in, f32[16,320]{1,0:T(8,128)} %get-tuple-element.7.gg_in, f32[40,128]{1,0:T(8,128)} %bitcast.5), custom_call_target="tpu_custom_call" | custom-call | tf_op jit(solution)/shard_map/pallas_call | solution.py:593
